TPU v7x, 512 devices: a whole 4x8x8 slice. The times are simulated.
512 devices in a mesh: group: 16 (over z_lo, x, core), expert: 32 (over y, z_hi).
Axes of the slice: x: 4, y: 8, z: 8 (z_hi: 4, z_lo: 2; z = z_hi * 2 + z_lo), core: 2. Of those that a mesh axis runs over, the one named last changes fastest.
Arguments:
- hidden: bfloat16 [3, 16384, 1024], P(None, ('group', 'expert')), may hold values from -6 to 6
- norm_gain: float32 [1024], replicated, may hold values from 0.1 to 1.9
- routes: int32 [3, 16384, 8], P(None, ('group', 'expert')), may hold values from 0 to 63, all different within a row; in each aligned block of 32 rows (0 to 31, 32 to 63, ..., all dimensions but the last counted through in order) at most 8 rows name the same one
- gates: float32 [3, 16384, 8], P(None, ('group', 'expert')), may hold values from 0.1 to 1
- switch: int32 [64], replicated, may hold values from 0 to 3
- experts_old: bfloat16 [64, 3, 384, 1024], P('expert', None, 'group'), may hold values from -0.25 to 0.25
- experts_new: bfloat16 [64, 3, 384, 1024], P('expert', None, 'group'), may hold values from -0.25 to 0.25
Outputs:
- mixed: bfloat16 [3, 16384, 1024], P(None, ('group', 'expert'))
Inputs may be any that keep to these rules, and one draw needn't show every extreme that they name: `routes`: in each step, no expert is named by more than 8 of one device's rows (aligned blocks of 32 rows); some expert is named by exactly 8 of them. A row names 8 different experts. `switch`: A value of 0 means the expert uses its new weights in every step; a value of 3 means it never does.
All inputs are finite; a program needn't handle non-finite values.
Results may differ from a plain program's by a relative error of at most 0.0065.
Values may be sent and summed in bfloat16 or wider, within the bound.
No kernel may reach another device: no remote copies, remote signals or barrier semaphores. Data moves between devices by JAX's collectives and lax.ppermute only.
A program may use at most 64 MiB of HBM per device.

v0:
```python
import jax
import jax.numpy as jnp
from jax import lax
from jax.sharding import PartitionSpec as P


def activate(rows_in, weights):
    gate_v = jnp.einsum("esd,efd->esf", rows_in, weights[:, 0], preferred_element_type=jnp.float32)
    up_v = jnp.einsum("esd,efd->esf", rows_in, weights[:, 1], preferred_element_type=jnp.float32)
    return (jax.nn.silu(gate_v) * up_v).astype(jnp.bfloat16)


def choose(flags, newer, older):
    shaped = flags.reshape((flags.shape[0],) + (1,) * (newer.ndim - 1))
    return jnp.where(shaped, newer, older)


def local(hidden, norm_gain, routes, gates, switch, experts_old, experts_new):
    steps, rows, width = hidden.shape
    exp_dev = experts_old.shape[0]
    members = lax.axis_size("expert")
    experts = exp_dev * members
    top = routes.shape[2]
    cap = 2 * rows * top // experts
    slots = experts * cap
    local_switch = lax.dynamic_slice_in_dim(switch, lax.axis_index("expert") * exp_dev, exp_dev, 0)
    xf = hidden.astype(jnp.float32)
    scale = lax.rsqrt(jnp.mean(xf * xf, axis=-1, keepdims=True) + 1e-06)
    normed = (xf * scale * norm_gain).astype(jnp.bfloat16)
    buffers = []
    combines = []
    for step in range(steps):
        flat = routes[step].reshape(rows * top)
        onehot = (flat[:, None] == jnp.arange(experts, dtype=jnp.int32)).astype(jnp.int32)
        before = jnp.cumsum(onehot, axis=0) - onehot
        rank = jnp.sum(before * onehot, axis=1)
        place = (flat * cap + rank).reshape(rows, top)
        match = place[:, :, None] == jnp.arange(slots, dtype=jnp.int32)
        spread = jnp.sum(match.astype(jnp.int32), axis=1).astype(jnp.bfloat16)
        combines.append(jnp.sum(jnp.where(match, gates[step][:, :, None], 0.0), axis=1))
        packed = lax.dot_general(
            spread, normed[step], (((0,), (0,)), ((), ())), preferred_element_type=jnp.float32
        )
        buffers.append(packed.astype(jnp.bfloat16).reshape(experts, cap, width))
    outgoing = jnp.stack(buffers, axis=1)
    received = jnp.stack(
        [
            lax.all_to_all(outgoing[:, step], "expert", split_axis=0, concat_axis=1, tiled=True)
            for step in range(steps)
        ],
        axis=1,
    )
    older = lax.all_gather(experts_old, "group", axis=2, tiled=True)
    newer = lax.all_gather(experts_new, "group", axis=2, tiled=True)
    parts = []
    for accumulate_step in range(steps):
        weights = choose(accumulate_step >= local_switch, newer, older)
        act = activate(received[:, accumulate_step], weights)
        parts.append(
            jnp.einsum("esf,efd->esd", act, weights[:, 2], preferred_element_type=jnp.float32)
        )
    produced = jnp.stack(parts, axis=1)
    produced = produced.astype(jnp.bfloat16)
    returned = jnp.stack(
        [
            lax.all_to_all(produced[:, step], "expert", split_axis=1, concat_axis=0, tiled=True)
            for step in range(steps)
        ],
        axis=1,
    )
    results = []
    for step in range(steps):
        outputs = returned[:, step].reshape(slots, width).astype(jnp.float32)
        total = jnp.dot(
            combines[step],
            outputs,
            precision=lax.Precision.HIGHEST,
            preferred_element_type=jnp.float32,
        )
        results.append((xf[step] + total).astype(jnp.bfloat16))
    return jnp.stack(results)


def solution(mesh):
    in_specs = (
        P(None, ("group", "expert"), None),
        P(),
        P(None, ("group", "expert"), None),
        P(None, ("group", "expert"), None),
        P(),
        P("expert", None, "group", None),
        P("expert", None, "group", None),
    )
    out_specs = P(None, ("group", "expert"), None)
    return jax.shard_map(local, mesh=mesh, in_specs=in_specs, out_specs=out_specs, check_vma=False)
```

profile of v0, /device:TPU:56, one launch (start us, length us, event | category | flops | bytes accessed | tf_op | source)
XLA Modules:
  0.0 297.5 jit_solution(7611862676021162958)
XLA Ops:
  6.5 1.7 copy.80
  8.3 1.7 copy.81
  16.0 15.7 %all-to-all-start = ((bf16[64,8,1024]{2,1,0:T(8,128)(2,1)}), bf16[64,8,1024]{2,1,0:T(8,128)(2,1)S(1)}, u32[]{:S(2)}, u32[]{:S(2)}) async-start(bf16[64,8,1024]{2,1,0:T(8,128)(2,1)} %fusion.12), calls=%async_computation | async-start | bytes 2097152 | tf_op jit(solution)/shard_map/all_to_all | solution.py:48
  34.7 26.7 %all-to-all-done = bf16[64,8,1024]{2,1,0:T(8,128)(2,1)S(1)} async-done(((bf16[64,8,1024]{2,1,0:T(8,128)(2,1)}), bf16[64,8,1024]{2,1,0:T(8,128)(2,1)S(1)}, u32[]{:S(2)}, u32[]{:S(2)}) %all-to-all-start) | async-done | bytes 1048608 | tf_op jit(solution)/shard_map/all_to_all | solution.py:48
  61.3 8.3 %all-to-all-start.2 = ((bf16[64,8,1024]{2,1,0:T(8,128)(2,1)}), bf16[64,8,1024]{2,1,0:T(8,128)(2,1)S(1)}, u32[]{:S(2)}, u32[]{:S(2)}) async-start(bf16[64,8,1024]{2,1,0:T(8,128)(2,1)} %fusion.13), calls=%async_computation.2 | async-start | bytes 2097152 | tf_op jit(solution)/shard_map/all_to_all | solution.py:48
  72.6 25.5 %all-to-all-done.2 = bf16[64,8,1024]{2,1,0:T(8,128)(2,1)S(1)} async-done(((bf16[64,8,1024]{2,1,0:T(8,128)(2,1)}), bf16[64,8,1024]{2,1,0:T(8,128)(2,1)S(1)}, u32[]{:S(2)}, u32[]{:S(2)}) %all-to-all-start.2) | async-done | bytes 1048608 | tf_op jit(solution)/shard_map/all_to_all | solution.py:48
  98.1 8.7 %all-to-all-start.4 = ((bf16[64,8,1024]{2,1,0:T(8,128)(2,1)}), bf16[64,8,1024]{2,1,0:T(8,128)(2,1)S(1)}, u32[]{:S(2)}, u32[]{:S(2)}) async-start(bf16[64,8,1024]{2,1,0:T(8,128)(2,1)} %fusion.14), calls=%async_computation.4 | async-start | bytes 2097152 | tf_op jit(solution)/shard_map/all_to_all | solution.py:48
  106.9 50.8 %all-gather.5.cloned.1.call-done = bf16[2,3,384,1024]{3,2,0,1:T(8,128)(2,1)} async-done(((bf16[2,3,24,1024]{3,2,0,1:T(8,128)(2,1)}), bf16[2,3,384,1024]{3,2,0,1:T(8,128)(2,1)}) %all-gather.5.cloned.1.call-update) | async-done | bytes 4718608 | tf_op jit(solution)/shard_map/all_gather | solution.py:53
  157.8 8.6 %broadcast_select_fusion.2 = (bf16[2,3,384,1024]{3,2,0,1:T(8,128)(2,1)S(1)}, bf16[2,3,384,1024]{3,2,0,1:T(8,128)(2,1)}, bf16[2,3,384,1024]{3,2,0,1:T(8,128)(2,1)}) fusion(bf16[2,3,384,1024]{3,2,0,1:T(8,128)(2,1)} %all-gather.3.cloned.1.call-done, bf16[2,3,384,1024]{3,2,0,1:T(8,128)(2,1)} %all-gather.5.cloned.1.call-done, ...), kind=kLoop, calls=%fused_computation.2 | loop fusion | flops 7077888 | bytes 23592966 | tf_op jit(solution)/shard_map/jit(_where)/select_n | solution.py:15
  166.4 2.2 copy-done
  170.2 4.4 %fusion.9 = bf16[2,256,1024]{2,1,0:T(8,128)(2,1)} fusion(bf16[2,3,384,1024]{3,2,0,1:T(8,128)(2,1)} %copy-done, bf16[32,2,8,1024]{3,2,1,0:T(8,128)(2,1)S(1)} %bitcast.211, f32[2,256,384]{2,1,0:T(8,128)} %fusion.8), kind=kOutput, calls=%fused_computation.21 | convolution fusion | flops 807010304 | bytes 6029312 | tf_op jit(solution)/shard_map/esf,efd->esd/dot_general | solution.py:60
  174.6 3.3 %copy.82 = bf16[2,256,1024]{2,0,1:T(2,128)(2,1)} copy(bf16[2,256,1024]{2,1,0:T(8,128)(2,1)} %fusion.9) | data formatting | bytes 2097152 | tf_op jit(solution)/shard_map/squeeze | solution.py:66
  177.9 10.1 %all-to-all-start.1 = ((bf16[2,256,1024]{2,0,1:T(2,128)(2,1)}), bf16[2,256,1024]{2,0,1:T(2,128)(2,1)S(1)}, u32[]{:S(2)}, u32[]{:S(2)}) async-start(bf16[2,256,1024]{2,0,1:T(2,128)(2,1)} %copy.82), calls=%async_computation.1 | async-start | bytes 2097152 | tf_op jit(solution)/shard_map/all_to_all | solution.py:66
  188.0 3.0 %fusion.5 = f32[2,256,384]{2,1,0:T(8,128)} fusion(bf16[2,3,384,1024]{3,2,0,1:T(8,128)(2,1)} %get-tuple-element.7, bf16[32,2,8,1024]{3,2,1,0:T(8,128)(2,1)S(1)} %bitcast.212), kind=kOutput, calls=%fused_computation.14 | convolution fusion | flops 402653184 | bytes 3407872 | tf_op jit(solution)/shard_map/esd,efd->esf/dot_general | solution.py:8
  191.0 4.4 %fusion.10 = bf16[2,256,1024]{2,1,0:T(8,128)(2,1)} fusion(bf16[2,3,384,1024]{3,2,0,1:T(8,128)(2,1)} %get-tuple-element.7, bf16[32,2,8,1024]{3,2,1,0:T(8,128)(2,1)S(1)} %bitcast.213, f32[2,256,384]{2,1,0:T(8,128)} %fusion.5), kind=kOutput, calls=%fused_computation.22 | convolution fusion | flops 807010304 | bytes 6029312 | tf_op jit(solution)/shard_map/esf,efd->esd/dot_general | solution.py:60
  195.4 3.3 %copy.89 = bf16[2,256,1024]{2,0,1:T(2,128)(2,1)} copy(bf16[2,256,1024]{2,1,0:T(8,128)(2,1)} %fusion.10) | data formatting | bytes 2097152 | tf_op jit(solution)/shard_map/squeeze | solution.py:66
  198.7 17.3 %all-to-all-done.1 = bf16[2,256,1024]{2,0,1:T(2,128)(2,1)S(1)} async-done(((bf16[2,256,1024]{2,0,1:T(2,128)(2,1)}), bf16[2,256,1024]{2,0,1:T(2,128)(2,1)S(1)}, u32[]{:S(2)}, u32[]{:S(2)}) %all-to-all-start.1) | async-done | bytes 1048608 | tf_op jit(solution)/shard_map/all_to_all | solution.py:66
  216.0 8.8 %all-to-all-start.3 = ((bf16[2,256,1024]{2,0,1:T(2,128)(2,1)}), bf16[2,256,1024]{2,0,1:T(2,128)(2,1)S(1)}, u32[]{:S(2)}, u32[]{:S(2)}) async-start(bf16[2,256,1024]{2,0,1:T(2,128)(2,1)} %copy.89), calls=%async_computation.3 | async-start | bytes 2097152 | tf_op jit(solution)/shard_map/all_to_all | solution.py:66
  224.8 3.0 %fusion.2 = f32[2,256,384]{2,1,0:T(8,128)} fusion(bf16[2,3,384,1024]{3,2,0,1:T(8,128)(2,1)} %get-tuple-element.6, bf16[32,2,8,1024]{3,2,1,0:T(8,128)(2,1)S(1)} %bitcast.214), kind=kOutput, calls=%fused_computation.8 | convolution fusion | flops 402653184 | bytes 3407872 | tf_op jit(solution)/shard_map/esd,efd->esf/dot_general | solution.py:8
  227.8 4.4 %fusion.11 = bf16[2,256,1024]{2,1,0:T(8,128)(2,1)} fusion(bf16[2,3,384,1024]{3,2,0,1:T(8,128)(2,1)} %get-tuple-element.6, bf16[32,2,8,1024]{3,2,1,0:T(8,128)(2,1)S(1)} %bitcast.215, f32[2,256,384]{2,1,0:T(8,128)} %fusion.2), kind=kOutput, calls=%fused_computation.23 | convolution fusion | flops 807010304 | bytes 6029312 | tf_op jit(solution)/shard_map/esf,efd->esd/dot_general | solution.py:60
  232.3 3.3 %copy.96 = bf16[2,256,1024]{2,0,1:T(2,128)(2,1)} copy(bf16[2,256,1024]{2,1,0:T(8,128)(2,1)} %fusion.11) | data formatting | bytes 2097152 | tf_op jit(solution)/shard_map/squeeze | solution.py:66
  235.6 15.9 %all-to-all-done.3 = bf16[2,256,1024]{2,0,1:T(2,128)(2,1)S(1)} async-done(((bf16[2,256,1024]{2,0,1:T(2,128)(2,1)}), bf16[2,256,1024]{2,0,1:T(2,128)(2,1)S(1)}, u32[]{:S(2)}, u32[]{:S(2)}) %all-to-all-start.3) | async-done | bytes 1048608 | tf_op jit(solution)/shard_map/all_to_all | solution.py:66
  251.5 8.7 %all-to-all-start.5 = ((bf16[2,256,1024]{2,0,1:T(2,128)(2,1)}), bf16[2,256,1024]{2,0,1:T(2,128)(2,1)S(1)}, u32[]{:S(2)}, u32[]{:S(2)}) async-start(bf16[2,256,1024]{2,0,1:T(2,128)(2,1)} %copy.96), calls=%async_computation.5 | async-start | bytes 2097152 | tf_op jit(solution)/shard_map/all_to_all | solution.py:66
  264.5 22.4 %all-to-all-done.5 = bf16[2,256,1024]{2,0,1:T(2,128)(2,1)S(1)} async-done(((bf16[2,256,1024]{2,0,1:T(2,128)(2,1)}), bf16[2,256,1024]{2,0,1:T(2,128)(2,1)S(1)}, u32[]{:S(2)}, u32[]{:S(2)}) %all-to-all-start.5) | async-done | bytes 1048608 | tf_op jit(solution)/shard_map/all_to_all | solution.py:66
  (82 shorter events, 21.6 us)
Async XLA Ops:
  6.5 100.4 %all-gather.3.cloned.1.call-start = ((), (), s32[]{:S(2)}) async-start(), calls=%async_computation.6 | async-start | bytes 5013504 | tf_op jit(solution)/shard_map/all_gather | solution.py:54
  8.3 149.5 %all-gather.5.cloned.1.call-start = ((), (), s32[]{:S(2)}) async-start(), calls=%async_computation.7 | async-start | bytes 5013504 | tf_op jit(solution)/shard_map/all_gather | solution.py:53
  16.0 90.9 %copy-start.6 = (s32[64]{0:T(128)S(1)}, s32[64]{0:T(128)}, u32[]{:S(2)}) copy-start(s32[64]{0:T(128)} %param.11) | copy-start | bytes 772
  16.0 45.4 %all-to-all-start = ((bf16[64,8,1024]{2,1,0:T(8,128)(2,1)}), bf16[64,8,1024]{2,1,0:T(8,128)(2,1)S(1)}, u32[]{:S(2)}, u32[]{:S(2)}) async-start(bf16[64,8,1024]{2,1,0:T(8,128)(2,1)} %fusion.12), calls=%async_computation | async-start | bytes 2097152 | tf_op jit(solution)/shard_map/all_to_all | solution.py:48
  61.3 36.8 %all-to-all-start.2 = ((bf16[64,8,1024]{2,1,0:T(8,128)(2,1)}), bf16[64,8,1024]{2,1,0:T(8,128)(2,1)S(1)}, u32[]{:S(2)}, u32[]{:S(2)}) async-start(bf16[64,8,1024]{2,1,0:T(8,128)(2,1)} %fusion.13), calls=%async_computation.2 | async-start | bytes 2097152 | tf_op jit(solution)/shard_map/all_to_all | solution.py:48
  98.1 79.8 %all-to-all-start.4 = ((bf16[64,8,1024]{2,1,0:T(8,128)(2,1)}), bf16[64,8,1024]{2,1,0:T(8,128)(2,1)S(1)}, u32[]{:S(2)}, u32[]{:S(2)}) async-start(bf16[64,8,1024]{2,1,0:T(8,128)(2,1)} %fusion.14), calls=%async_computation.4 | async-start | bytes 2097152 | tf_op jit(solution)/shard_map/all_to_all | solution.py:48
  166.4 2.2 copy-start
  177.9 38.1 %all-to-all-start.1 = ((bf16[2,256,1024]{2,0,1:T(2,128)(2,1)}), bf16[2,256,1024]{2,0,1:T(2,128)(2,1)S(1)}, u32[]{:S(2)}, u32[]{:S(2)}) async-start(bf16[2,256,1024]{2,0,1:T(2,128)(2,1)} %copy.82), calls=%async_computation.1 | async-start | bytes 2097152 | tf_op jit(solution)/shard_map/all_to_all | solution.py:66
  216.0 35.4 %all-to-all-start.3 = ((bf16[2,256,1024]{2,0,1:T(2,128)(2,1)}), bf16[2,256,1024]{2,0,1:T(2,128)(2,1)S(1)}, u32[]{:S(2)}, u32[]{:S(2)}) async-start(bf16[2,256,1024]{2,0,1:T(2,128)(2,1)} %copy.89), calls=%async_computation.3 | async-start | bytes 2097152 | tf_op jit(solution)/shard_map/all_to_all | solution.py:66
  227.8 32.3 %copy-start.1 = (bf16[3,32,1024]{2,1,0:T(8,128)(2,1)S(1)}, bf16[3,32,1024]{2,1,0:T(8,128)(2,1)}, u32[]{:S(2)}) copy-start(bf16[3,32,1024]{2,1,0:T(8,128)(2,1)} %param.7) | copy-start | bytes 589828
  232.3 28.7 %copy-start.5 = (f32[3,32,8]{1,2,0:T(8,128)S(1)}, f32[3,32,8]{1,2,0:T(8,128)}, u32[]{:S(2)}) copy-start(f32[3,32,8]{1,2,0:T(8,128)} %param.10) | copy-start | bytes 9220
  251.5 35.4 %all-to-all-start.5 = ((bf16[2,256,1024]{2,0,1:T(2,128)(2,1)}), bf16[2,256,1024]{2,0,1:T(2,128)(2,1)S(1)}, u32[]{:S(2)}, u32[]{:S(2)}) async-start(bf16[2,256,1024]{2,0,1:T(2,128)(2,1)} %copy.96), calls=%async_computation.5 | async-start | bytes 2097152 | tf_op jit(solution)/shard_map/all_to_all | solution.py:66
  264.1 23.1 %copy-start.2 = (f32[3,32,1024]{2,1,0:T(8,128)S(1)}, f32[3,32,1024]{2,1,0:T(8,128)}, u32[]{:S(2)}) copy-start(f32[3,32,1024]{2,1,0:T(8,128)} %convert_element_type.76) | copy-start | bytes 1179652
  286.9 1.8 copy-start.4
  286.9 2.5 copy-start.3
Sparse Core Ops, SparseCore 0:
  9.5 90.8 all-gather.2
  102.4 55.2 all-gather.4
where the time goes:
time: 301 us; the launch traced here: 297 us
  waiting for transfers between devices  159 us (53%)
  starting transfers between devices  60.3 us (20%)
  matrix products  27.9 us (9%)
  local copies, waits for them, and re-layouts  19.2 us (6%)
  other arithmetic  17.9 us (6%)
  between operations  13.7 us (5%)
    all_to_all x3, waiting for transfers between devices, local(): lax.all_to_all(produced[:, step], 'expert', split_axis=1, concat_axis=0,...  55.6 us
    all_to_all x3, waiting for transfers between devices, local(): lax.all_to_all(outgoing[:, step], 'expert', split_axis=0, concat_axis=1,...  52.1 us
    all_gather x1, waiting for transfers between devices, local(): older = lax.all_gather(experts_old, 'group', axis=2, tiled=True)  50.8 us
    all_to_all x3, starting transfers between devices, local(): lax.all_to_all(outgoing[:, step], 'expert', split_axis=0, concat_axis=1,...  32.7 us
    all_to_all x3, starting transfers between devices, local(): lax.all_to_all(produced[:, step], 'expert', split_axis=1, concat_axis=0,...  27.6 us
    dot_general x3, matrix products, local(): jnp.einsum('esf,efd->esd', act, weights[:, 2], preferred_element_type=jnp...  13.2 us
    squeeze x3, local copies, waits for them, and re-layouts, local(): produced[:, step]  9.9 us
    select_n x1, other arithmetic, choose(): return jnp.where(shaped, newer, older)  8.62 us
  transfers between devices with their start and end apart: 8, of which 6 were waited for; matrix products, arithmetic and copies ran while one was open for 19% of the time, Pallas kernels for 0%

commit v1 on v0

v1 whole, which is shorter than its diff:
```python
import jax
import jax.numpy as jnp
from jax import lax
from jax.experimental import pallas as pl
from jax.experimental.pallas import tpu as pltpu
from jax.sharding import PartitionSpec as P

CAP = 8
F32 = jnp.float32
BF16 = jnp.bfloat16


def slot_mask(routes, experts):
    rows, top = routes.shape
    slots = experts * CAP
    lane = lax.broadcasted_iota(jnp.int32, (rows, slots), 1)
    owner = lane >> 3
    named = routes[:, 0:1] == owner
    for k in range(1, top):
        named = named | (routes[:, k : k + 1] == owner)
    earlier = lax.broadcasted_iota(jnp.int32, (rows, rows), 1) < lax.broadcasted_iota(
        jnp.int32, (rows, rows), 0
    )
    rank = jnp.dot(
        earlier.astype(F32).astype(BF16), named.astype(F32).astype(BF16), preferred_element_type=F32
    )
    return named & (rank == (lane & 7).astype(F32))


def pack_kernel(hidden_ref, gain_ref, routes_ref, out_ref):
    steps, rows, width = hidden_ref.shape
    members, _, per, _ = out_ref.shape
    for step in range(steps):
        xf = hidden_ref[step].astype(F32)
        scale = lax.rsqrt(jnp.mean(xf * xf, axis=-1, keepdims=True) + 1e-06)
        normed = (xf * scale * gain_ref[...]).astype(BF16)
        spread = slot_mask(routes_ref[step], members * per // CAP).astype(F32).astype(BF16)
        packed = lax.dot_general(
            spread, normed, (((0,), (0,)), ((), ())), preferred_element_type=F32
        )
        out_ref[:, step] = packed.astype(BF16).reshape(members, per, width)


def weigh_kernel(routes_ref, gates_ref, out_ref):
    steps, rows, top = routes_ref.shape
    slots = out_ref.shape[2]
    for step in range(steps):
        routes = routes_ref[step]
        gates = gates_ref[step]
        mask = slot_mask(routes, slots // CAP)
        owner = lax.broadcasted_iota(jnp.int32, (rows, slots), 1) >> 3
        weight = jnp.zeros((rows, slots), F32)
        for k in range(top):
            weight = jnp.where(routes[:, k : k + 1] == owner, gates[:, k : k + 1], weight)
        weight = jnp.where(mask, weight, 0.0)
        high = weight.astype(BF16)
        rest = weight - high.astype(F32)
        mid = rest.astype(BF16)
        low = (rest - mid.astype(F32)).astype(BF16)
        out_ref[step, 0:rows] = high
        out_ref[step, rows : 2 * rows] = mid
        out_ref[step, 2 * rows : 3 * rows] = low


def expert_kernel(version_ref, rows_ref, weights_ref, out_ref, held_ref):
    members, _, per, width = rows_ref.shape
    e = pl.program_id(1)
    both = rows_ref[:, 0].astype(F32)
    nt = (((1,), (1,)), ((), ()))

    def expert(mine):
        rows_in = mine.reshape(members * CAP, width).astype(BF16)
        gate_v = lax.dot_general(rows_in, weights_ref[0, 0, 0], nt, preferred_element_type=F32)
        up_v = lax.dot_general(rows_in, weights_ref[0, 0, 1], nt, preferred_element_type=F32)
        act = (gate_v / (1.0 + jnp.exp(-gate_v)) * up_v).astype(BF16)
        made = jnp.dot(act, weights_ref[0, 0, 2], preferred_element_type=F32)
        return made.reshape(members, CAP, width)

    @pl.when(e == 0)
    def _():
        held_ref[...] = expert(both[:, :CAP])

    @pl.when(e == 1)
    def _():
        made = expert(both[:, CAP:])
        out_ref[:, 0] = jnp.concatenate([held_ref[...], made], axis=1).astype(BF16)


def combine_kernel(hidden_ref, weights_ref, back_ref, out_ref):
    steps, rows, width = hidden_ref.shape
    members, _, per, _ = back_ref.shape
    for step in range(steps):
        outputs = back_ref[:, step].reshape(members * per, width)
        parts = jnp.dot(weights_ref[step], outputs, preferred_element_type=F32)
        total = parts[2 * rows :] + parts[rows : 2 * rows] + parts[:rows]
        out_ref[step] = (hidden_ref[step].astype(F32) + total).astype(BF16)


def local(hidden, norm_gain, routes, gates, switch, experts_old, experts_new):
    steps, rows, width = hidden.shape
    exp_dev, mats, shard, _ = experts_old.shape
    members = lax.axis_size("expert")
    groups = lax.axis_size("group")
    per = exp_dev * CAP
    slots = members * per
    big = pltpu.CompilerParams(vmem_limit_bytes=48 * 1024 * 1024)

    both = jnp.stack([experts_old, experts_new])
    weights = lax.all_gather(both, "group", axis=3, tiled=True)

    outgoing = pl.pallas_call(
        pack_kernel,
        out_shape=jax.ShapeDtypeStruct((members, steps, per, width), BF16),
        compiler_params=big,
        name="pack",
    )(hidden, norm_gain.reshape(1, width), routes)
    received = lax.all_to_all(outgoing, "expert", split_axis=0, concat_axis=0, tiled=True)
    weigh = pl.pallas_call(
        weigh_kernel,
        out_shape=jax.ShapeDtypeStruct((steps, 3 * rows, slots), BF16),
        compiler_params=big,
        name="weigh",
    )(routes, gates)

    mine = lax.dynamic_slice_in_dim(switch, lax.axis_index("expert") * exp_dev, exp_dev, 0)
    version = (jnp.arange(steps, dtype=jnp.int32)[:, None] >= mine).astype(jnp.int32).reshape(-1)
    produced = pl.pallas_call(
        expert_kernel,
        grid_spec=pltpu.PrefetchScalarGridSpec(
            num_scalar_prefetch=1,
            grid=(steps, exp_dev),
            in_specs=[
                pl.BlockSpec((members, 1, per, width), lambda s, e, v: (0, s, 0, 0)),
                pl.BlockSpec(
                    (1, 1, mats, shard * groups, width), lambda s, e, v: (v[s * 2 + e], e, 0, 0, 0)
                ),
            ],
            out_specs=pl.BlockSpec((members, 1, per, width), lambda s, e, v: (0, s, 0, 0)),
            scratch_shapes=[pltpu.VMEM((members, CAP, width), F32)],
        ),
        out_shape=jax.ShapeDtypeStruct((members, steps, per, width), BF16),
        compiler_params=big,
        name="experts",
    )(version, received, weights)
    returned = lax.all_to_all(produced, "expert", split_axis=0, concat_axis=0, tiled=True)
    return pl.pallas_call(
        combine_kernel,
        out_shape=jax.ShapeDtypeStruct((steps, rows, width), BF16),
        compiler_params=big,
        name="combine",
    )(hidden, weigh, returned)


def solution(mesh):
    in_specs = (
        P(None, ("group", "expert"), None),
        P(),
        P(None, ("group", "expert"), None),
        P(None, ("group", "expert"), None),
        P(),
        P("expert", None, "group", None),
        P("expert", None, "group", None),
    )
    out_specs = P(None, ("group", "expert"), None)
    return jax.shard_map(local, mesh=mesh, in_specs=in_specs, out_specs=out_specs, check_vma=False)
```

time: 301 us -> 279 us (0.927)
  the two profiles are of different devices: /device:TPU:56 before, /device:TPU:218 now
where the time goes in v1:
time: 279 us
  waiting for transfers between devices  208 us (75%)
  starting transfers between devices  33.8 us (12%)
  Pallas kernels  16.5 us (6%)
  between operations  13.5 us (5%)
  local copies, waits for them, and re-layouts  5.2 us (2%)
    all_to_all x1, waiting for transfers between devices, local(): lax.all_to_all(produced, 'expert', split_axis=0, concat_axis=0, tiled=True)  94.2 us
    all_to_all x1, waiting for transfers between devices, local(): lax.all_to_all(outgoing, 'expert', split_axis=0, concat_axis=0, tiled=True)  82.7 us
    all_gather x1, waiting for transfers between devices, local(): weights = lax.all_gather(both, 'group', axis=3, tiled=True)  30.9 us
    all_to_all x1, starting transfers between devices, local(): lax.all_to_all(produced, 'expert', split_axis=0, concat_axis=0, tiled=True)  20.4 us
    all_to_all x1, starting transfers between devices, local(): lax.all_to_all(outgoing, 'expert', split_axis=0, concat_axis=0, tiled=True)  13.4 us
    pallas_call x1, Pallas kernels, local(): pl.pallas_call(expert_kernel, grid_spec=pltpu.PrefetchScalarGridSpec(num_...  11.3 us
  transfers between devices with their start and end apart: 3, of which 3 were waited for; matrix products, arithmetic and copies ran while one was open for 0% of the time, Pallas kernels for 1%

profile of v1, /device:TPU:218, one launch (start us, length us, event | category | flops | bytes accessed | tf_op | source)
XLA Modules:
  0.0 278.7 jit_solution(7706843633436205037)
XLA Ops:
  6.5 0.0 all-gather.2.cloned.1.call-start
  6.5 2.0 pad_maximum_fusion
  8.5 0.0 all-gather.2.cloned.1.call-update
  8.5 0.8 copy.11.routes_ref
  9.3 0.9 copy-done.1
  10.2 0.7 copy-done.3
  10.9 3.4 %pack.1 = bf16[32,3,16,1024]{3,2,1,0:T(8,128)(2,1)} custom-call(bf16[3,32,1024]{2,1,0:T(8,128)(2,1)S(1)} %copy-done.1, f32[1,1024]{1,0:T(1,128)S(1)} %bitcast.3, s32[3,32,8]{2,1,0:T(8,128)S(1)} %copy.11.routes_ref), custom_call_target="tpu_custom_call" | custom-call | tf_op jit(solution)/shard_map/pack/pallas_call | solution.py:111
  14.3 13.4 %all-to-all-start = ((bf16[32,3,16,1024]{3,2,1,0:T(8,128)(2,1)}), bf16[32,3,16,1024]{3,2,1,0:T(8,128)(2,1)S(1)}, u32[]{:S(2)}, u32[]{:S(2)}) async-start(bf16[32,3,16,1024]{3,2,1,0:T(8,128)(2,1)} %pack.1), calls=%async_computation | async-start | bytes 6291456 | tf_op jit(solution)/shard_map/all_to_all | solution.py:117
  27.7 0.0 copy-done.6
  27.7 0.1 dynamic_slice.3
  27.8 0.1 reshape.11.version_ref
  27.9 82.7 %all-to-all-done.rows_ref = bf16[32,3,16,1024]{3,2,1,0:T(8,128)(2,1)S(1)} async-done(((bf16[32,3,16,1024]{3,2,1,0:T(8,128)(2,1)}), bf16[32,3,16,1024]{3,2,1,0:T(8,128)(2,1)S(1)}, u32[]{:S(2)}, u32[]{:S(2)}) %all-to-all-start) | async-done | bytes 3145760 | tf_op jit(solution)/shard_map/all_to_all | solution.py:117
  110.6 30.9 %all-gather.2.cloned.1.call-done.weights_ref = bf16[2,2,3,384,1024]{4,3,2,1,0:T(8,128)(2,1)} async-done(((bf16[2,2,3,24,1024]{4,3,2,1,0:T(8,128)(2,1)}), bf16[2,2,3,384,1024]{4,3,2,1,0:T(8,128)(2,1)}) %all-gather.2.cloned.1.call-update) | async-done | bytes 9437200 | tf_op jit(solution)/shard_map/all_gather | solution.py:109
  141.5 0.0 copy-done.4
  141.5 11.3 %experts.1 = bf16[32,3,16,1024]{3,2,1,0:T(8,128)(2,1)S(1)} custom-call(s32[6]{0:T(128)S(1)} %reshape.11.version_ref, bf16[32,3,16,1024]{3,2,1,0:T(8,128)(2,1)} %copy-done.4, bf16[2,2,3,384,1024]{4,3,2,1,0:T(8,128)(2,1)} %all-gather.2.cloned.1.call-done.weights_ref), custom_call_target="tpu_custom_call" | custom-call | tf_op jit(solution)/shard_map/experts/pallas_call | solution.py:127
  152.8 0.0 copy-start
  152.8 1.6 copy-done
  154.5 20.4 %all-to-all-start.1 = ((bf16[32,3,16,1024]{3,2,1,0:T(8,128)(2,1)}), bf16[32,3,16,1024]{3,2,1,0:T(8,128)(2,1)S(1)}, u32[]{:S(2)}, u32[]{:S(2)}) async-start(bf16[32,3,16,1024]{3,2,1,0:T(8,128)(2,1)} %copy-done), calls=%async_computation.1 | async-start | bytes 6291456 | tf_op jit(solution)/shard_map/all_to_all | solution.py:145
  174.8 0.0 copy-done.5
  174.9 0.1 copy.12.gates_ref
  174.9 0.5 weigh.1.weights_ref
  175.4 94.2 %all-to-all-done.1.back_ref = bf16[32,3,16,1024]{3,2,1,0:T(8,128)(2,1)S(1)} async-done(((bf16[32,3,16,1024]{3,2,1,0:T(8,128)(2,1)}), bf16[32,3,16,1024]{3,2,1,0:T(8,128)(2,1)S(1)}, u32[]{:S(2)}, u32[]{:S(2)}) %all-to-all-start.1) | async-done | bytes 3145760 | tf_op jit(solution)/shard_map/all_to_all | solution.py:145
  269.7 0.9 copy-done.2
  270.6 1.3 combine.1
  (7 shorter events, 0.0 us)
Async XLA Ops:
  6.5 135.0 %all-gather.2.cloned.1.call-start = ((), (), s32[]{:S(2)}) async-start(), calls=%async_computation.2 | async-start | bytes 10027008 | tf_op jit(solution)/shard_map/all_gather | solution.py:109
  9.3 0.9 copy-start.1
  10.2 0.7 copy-start.3
  14.3 13.4 %copy-start.6 = (s32[64]{0:T(128)S(1)}, s32[64]{0:T(128)}, u32[]{:S(2)}) copy-start(s32[64]{0:T(128)} %param.11) | copy-start | bytes 772
  14.3 96.3 %all-to-all-start = ((bf16[32,3,16,1024]{3,2,1,0:T(8,128)(2,1)}), bf16[32,3,16,1024]{3,2,1,0:T(8,128)(2,1)S(1)}, u32[]{:S(2)}, u32[]{:S(2)}) async-start(bf16[32,3,16,1024]{3,2,1,0:T(8,128)(2,1)} %pack.1), calls=%async_computation | async-start | bytes 6291456 | tf_op jit(solution)/shard_map/all_to_all | solution.py:117
  110.6 30.9 %copy-start.4 = (bf16[32,3,16,1024]{3,2,1,0:T(8,128)(2,1)}, bf16[32,3,16,1024]{3,2,1,0:T(8,128)(2,1)S(1)}, u32[]{:S(2)}) copy-start(bf16[32,3,16,1024]{3,2,1,0:T(8,128)(2,1)S(1)} %all-to-all-done.rows_ref) | copy-start | bytes 9437188
  152.8 1.6 copy-start
  154.5 20.4 %copy-start.5 = (f32[3,32,8]{1,2,0:T(8,128)S(1)}, f32[3,32,8]{1,2,0:T(8,128)}, u32[]{:S(2)}) copy-start(f32[3,32,8]{1,2,0:T(8,128)} %param.10) | copy-start | bytes 9220
  154.5 115.2 %all-to-all-start.1 = ((bf16[32,3,16,1024]{3,2,1,0:T(8,128)(2,1)}), bf16[32,3,16,1024]{3,2,1,0:T(8,128)(2,1)S(1)}, u32[]{:S(2)}, u32[]{:S(2)}) async-start(bf16[32,3,16,1024]{3,2,1,0:T(8,128)(2,1)} %copy-done), calls=%async_computation.1 | async-start | bytes 6291456 | tf_op jit(solution)/shard_map/all_to_all | solution.py:145
  269.7 0.9 copy-start.2
Sparse Core Ops, SparseCore 0:
  9.5 132.0 all-gather.1

commit v2 on v1

--- a/solution.py
+++ b/solution.py
@@ -27,39 +27,34 @@
     return named & (rank == (lane & 7).astype(F32))
 
 
-def pack_kernel(hidden_ref, gain_ref, routes_ref, out_ref):
+def pack_kernel(hidden_ref, gain_ref, routes_ref, gates_ref, out_ref, weights_ref):
     steps, rows, width = hidden_ref.shape
     members, _, per, _ = out_ref.shape
+    slots = members * per
+    owner = lax.broadcasted_iota(jnp.int32, (rows, slots), 1) >> 3
     for step in range(steps):
         xf = hidden_ref[step].astype(F32)
         scale = lax.rsqrt(jnp.mean(xf * xf, axis=-1, keepdims=True) + 1e-06)
         normed = (xf * scale * gain_ref[...]).astype(BF16)
-        spread = slot_mask(routes_ref[step], members * per // CAP).astype(F32).astype(BF16)
+        routes = routes_ref[step]
+        gates = gates_ref[step]
+        mask = slot_mask(routes, slots // CAP)
+        spread = mask.astype(F32).astype(BF16)
         packed = lax.dot_general(
             spread, normed, (((0,), (0,)), ((), ())), preferred_element_type=F32
         )
         out_ref[:, step] = packed.astype(BF16).reshape(members, per, width)
-
-
-def weigh_kernel(routes_ref, gates_ref, out_ref):
-    steps, rows, top = routes_ref.shape
-    slots = out_ref.shape[2]
-    for step in range(steps):
-        routes = routes_ref[step]
-        gates = gates_ref[step]
-        mask = slot_mask(routes, slots // CAP)
-        owner = lax.broadcasted_iota(jnp.int32, (rows, slots), 1) >> 3
         weight = jnp.zeros((rows, slots), F32)
-        for k in range(top):
+        for k in range(routes.shape[1]):
             weight = jnp.where(routes[:, k : k + 1] == owner, gates[:, k : k + 1], weight)
         weight = jnp.where(mask, weight, 0.0)
         high = weight.astype(BF16)
         rest = weight - high.astype(F32)
         mid = rest.astype(BF16)
         low = (rest - mid.astype(F32)).astype(BF16)
-        out_ref[step, 0:rows] = high
-        out_ref[step, rows : 2 * rows] = mid
-        out_ref[step, 2 * rows : 3 * rows] = low
+        weights_ref[step, 0:rows] = high
+        weights_ref[step, rows : 2 * rows] = mid
+        weights_ref[step, 2 * rows : 3 * rows] = low
 
 
 def expert_kernel(version_ref, rows_ref, weights_ref, out_ref, held_ref):
@@ -105,22 +100,30 @@
     slots = members * per
     big = pltpu.CompilerParams(vmem_limit_bytes=48 * 1024 * 1024)
 
-    both = jnp.stack([experts_old, experts_new])
-    weights = lax.all_gather(both, "group", axis=3, tiled=True)
-
-    outgoing = pl.pallas_call(
+    half = groups // 2
+    swap = [(i, (i + half) % groups) for i in range(groups)]
+    planes = [list(range(half)), list(range(half, groups))]
+    others = [lax.ppermute(shard_of, "group", swap) for shard_of in (experts_old, experts_new)]
+    outgoing, weigh = pl.pallas_call(
         pack_kernel,
-        out_shape=jax.ShapeDtypeStruct((members, steps, per, width), BF16),
+        out_shape=(
+            jax.ShapeDtypeStruct((members, steps, per, width), BF16),
+            jax.ShapeDtypeStruct((steps, 3 * rows, slots), BF16),
+        ),
         compiler_params=big,
+        cost_estimate=pl.CostEstimate(
+            flops=2 * steps * rows * slots * width, bytes_accessed=4 << 20, transcendentals=0
+        ),
         name="pack",
-    )(hidden, norm_gain.reshape(1, width), routes)
+    )(hidden, norm_gain.reshape(1, width), routes, gates)
+    others, outgoing = lax.optimization_barrier((others, outgoing))
+    shards = [
+        jnp.concatenate(pair, axis=2) for pair in zip((experts_old, experts_new), others)
+    ]
+    weights = lax.all_gather(
+        jnp.stack(shards), "group", axis=3, tiled=True, axis_index_groups=planes
+    )
     received = lax.all_to_all(outgoing, "expert", split_axis=0, concat_axis=0, tiled=True)
-    weigh = pl.pallas_call(
-        weigh_kernel,
-        out_shape=jax.ShapeDtypeStruct((steps, 3 * rows, slots), BF16),
-        compiler_params=big,
-        name="weigh",
-    )(routes, gates)
 
     mine = lax.dynamic_slice_in_dim(switch, lax.axis_index("expert") * exp_dev, exp_dev, 0)
     version = (jnp.arange(steps, dtype=jnp.int32)[:, None] >= mine).astype(jnp.int32).reshape(-1)

time: 279 us -> 244 us (0.87)
  the two profiles are of different devices: /device:TPU:218 before, /device:TPU:56 now
where the time goes in v2:
time: 244 us; the launch traced here: 243 us
  blocking collectives  98 us (40%)
  waiting for transfers between devices  87.3 us (36%)
  starting transfers between devices  21.1 us (9%)
  Pallas kernels  16.1 us (7%)
  between operations  13.5 us (6%)
  local copies, waits for them, and re-layouts  5.02 us (2%)
    all_to_all x1, blocking collectives, local(): lax.all_to_all(produced, 'expert', split_axis=0, concat_axis=0, tiled=True)  98 us
    all_to_all x1, waiting for transfers between devices, local(): lax.all_to_all(outgoing, 'expert', split_axis=0, concat_axis=0, tiled=True)  82.3 us
    all_to_all x1, starting transfers between devices, local(): lax.all_to_all(outgoing, 'expert', split_axis=0, concat_axis=0, tiled=True)  14.9 us
    pallas_call x1, Pallas kernels, local(): pl.pallas_call(expert_kernel, grid_spec=pltpu.PrefetchScalarGridSpec(num_...  11.3 us
    ppermute x2, starting transfers between devices, local(): lax.ppermute(shard_of, 'group', swap)  6.19 us
    ppermute x2, waiting for transfers between devices, local(): lax.ppermute(shard_of, 'group', swap)  4.97 us
  transfers between devices with their start and end apart: 4, of which 2 were waited for; matrix products, arithmetic and copies ran while one was open for 1% of the time, Pallas kernels for 1%

profile of v2, /device:TPU:56, one launch (start us, length us, event | category | flops | bytes accessed | tf_op | source)
XLA Modules:
  0.0 243.4 jit_solution(8163388182952098929)
XLA Ops:
  6.5 0.0 all-gather.2.cloned.1.call-start
  6.5 4.3 %collective-permute-start = (bf16[2,3,24,1024]{3,2,1,0:T(8,128)(2,1)}, bf16[2,3,24,1024]{3,2,1,0:T(8,128)(2,1)S(1)}, u32[]{:S(2)}, u32[]{:S(2)}) collective-permute-start(bf16[2,3,24,1024]{3,2,1,0:T(8,128)(2,1)} %param.12), channel_id=1, source_target_pairs={{0,256},{32,288},{64,320},{96,352},{128,384},{160,416},{192,448},{... | collective-permute-start | bytes 884744 | tf_op jit(solution)/shard_map/ppermute | solution.py:106
  10.8 1.9 collective-permute-start.1
  12.7 0.8 copy.10.routes_ref
  13.5 0.8 copy.11.gates_ref
  14.3 0.9 copy-done
  15.3 0.7 copy-done.2
  15.9 3.4 %pack.1 = (bf16[32,3,16,1024]{3,2,1,0:T(8,128)(2,1)}, bf16[3,96,512]{2,1,0:T(8,128)(2,1)S(1)}) custom-call(bf16[3,32,1024]{2,1,0:T(8,128)(2,1)S(1)} %copy-done, f32[1,1024]{1,0:T(1,128)S(1)} %bitcast.5, s32[3,32,8]{2,1,0:T(8,128)S(1)} %copy.10.routes_ref, f32[3,32,8]{2,1,0:T(8,128)S(1)} %copy.11.gates_ref), custom_call_target="tpu_custom_call" | custom-call | flops 100663296 | bytes 4194304 | tf_op jit(solution)/shard_map/pack/pallas_call | solution.py:107
  19.4 0.0 collective-permute-done
  19.4 5.0 %collective-permute-done.1 = bf16[2,3,24,1024]{3,2,1,0:T(8,128)(2,1)S(1)} collective-permute-done((bf16[2,3,24,1024]{3,2,1,0:T(8,128)(2,1)}, bf16[2,3,24,1024]{3,2,1,0:T(8,128)(2,1)S(1)}, u32[]{:S(2)}, u32[]{:S(2)}) %collective-permute-start.1) | collective-permute-done | bytes 294944 | tf_op jit(solution)/shard_map/ppermute | solution.py:106
  24.3 1.2 maximum_bitcast_fusion
  25.5 1.2 pad_maximum_fusion
  26.7 0.0 all-gather.2.cloned.1.call-update
  26.7 0.0 copy-start.4
  26.7 14.9 %all-to-all-start = ((bf16[32,3,16,1024]{3,2,1,0:T(8,128)(2,1)}), bf16[32,3,16,1024]{3,2,1,0:T(8,128)(2,1)S(1)}, u32[]{:S(2)}, u32[]{:S(2)}) async-start(bf16[32,3,16,1024]{3,2,1,0:T(8,128)(2,1)} %get-tuple-element.12), calls=%async_computation | async-start | bytes 6291456 | tf_op jit(solution)/shard_map/all_to_all | solution.py:126
  41.7 0.1 dynamic_slice.3
  41.8 0.1 reshape.11.version_ref
  41.8 82.3 %all-to-all-done.rows_ref = bf16[32,3,16,1024]{3,2,1,0:T(8,128)(2,1)S(1)} async-done(((bf16[32,3,16,1024]{3,2,1,0:T(8,128)(2,1)}), bf16[32,3,16,1024]{3,2,1,0:T(8,128)(2,1)S(1)}, u32[]{:S(2)}, u32[]{:S(2)}) %all-to-all-start) | async-done | bytes 3145760 | tf_op jit(solution)/shard_map/all_to_all | solution.py:126
  124.2 1.7 copy-done.3
  125.8 11.3 %experts.1 = bf16[32,3,16,1024]{3,2,1,0:T(8,128)(2,1)S(1)} custom-call(s32[6]{0:T(128)S(1)} %reshape.11.version_ref, bf16[32,3,16,1024]{3,2,1,0:T(8,128)(2,1)} %copy-done.3, bf16[2,2,3,384,1024]{4,3,2,1,0:T(8,128)(2,1)} %all-gather.2.cloned.1.call-done.weights_ref), custom_call_target="tpu_custom_call" | custom-call | tf_op jit(solution)/shard_map/experts/pallas_call | solution.py:130
  137.1 0.0 copy-start.1
  137.1 98.0 %all_to_all.10.back_ref = bf16[32,3,16,1024]{3,2,1,0:T(8,128)(2,1)S(1)} all-to-all(bf16[32,3,16,1024]{3,2,1,0:T(8,128)(2,1)S(1)} %experts.1), channel_id=1, replica_groups=mesh['group'=16,'expert'=32] {'expert'}, dimensions={0} | all-to-all | bytes 6291456 | tf_op jit(solution)/shard_map/all_to_all | solution.py:148
  235.1 0.0 copy-done.1
  235.1 1.4 combine.1
  (6 shorter events, 0.0 us)
Async XLA Ops:
  6.5 117.6 %all-gather.2.cloned.1.call-start = ((), (), s32[]{:S(2)}) async-start(), calls=%async_computation.2 | async-start | bytes 10616832 | tf_op jit(solution)/shard_map/all_gather | solution.py:123
  6.5 12.8 %collective-permute-start = (bf16[2,3,24,1024]{3,2,1,0:T(8,128)(2,1)}, bf16[2,3,24,1024]{3,2,1,0:T(8,128)(2,1)S(1)}, u32[]{:S(2)}, u32[]{:S(2)}) collective-permute-start(bf16[2,3,24,1024]{3,2,1,0:T(8,128)(2,1)} %param.12), channel_id=1, source_target_pairs={{0,256},{32,288},{64,320},{96,352},{128,384},{160,416},{192,448},{... | collective-permute-start | bytes 884744 | tf_op jit(solution)/shard_map/ppermute | solution.py:106
  10.8 13.5 %collective-permute-start.1 = (bf16[2,3,24,1024]{3,2,1,0:T(8,128)(2,1)}, bf16[2,3,24,1024]{3,2,1,0:T(8,128)(2,1)S(1)}, u32[]{:S(2)}, u32[]{:S(2)}) collective-permute-start(bf16[2,3,24,1024]{3,2,1,0:T(8,128)(2,1)} %param.13), channel_id=1, source_target_pairs={{0,256},{32,288},{64,320},{96,352},{128,384},{160,416},{192,448},{... | collective-permute-start | bytes 884744 | tf_op jit(solution)/shard_map/ppermute | solution.py:106
  14.3 0.9 copy-start
  15.3 0.7 copy-start.2
  26.7 15.0 %copy-start.4 = (s32[64]{0:T(128)S(1)}, s32[64]{0:T(128)}, u32[]{:S(2)}) copy-start(s32[64]{0:T(128)} %param.11) | copy-start | bytes 772
  26.7 97.5 %all-to-all-start = ((bf16[32,3,16,1024]{3,2,1,0:T(8,128)(2,1)}), bf16[32,3,16,1024]{3,2,1,0:T(8,128)(2,1)S(1)}, u32[]{:S(2)}, u32[]{:S(2)}) async-start(bf16[32,3,16,1024]{3,2,1,0:T(8,128)(2,1)} %get-tuple-element.12), calls=%async_computation | async-start | bytes 6291456 | tf_op jit(solution)/shard_map/all_to_all | solution.py:126
  124.2 1.7 copy-start.3
  137.1 98.0 %copy-start.1 = (bf16[3,32,1024]{2,1,0:T(8,128)(2,1)S(1)}, bf16[3,32,1024]{2,1,0:T(8,128)(2,1)}, u32[]{:S(2)}) copy-start(bf16[3,32,1024]{2,1,0:T(8,128)(2,1)} %hidden_ref.3) | copy-start | bytes 589828
Sparse Core Ops, SparseCore 0:
  26.8 62.7 all-gather.1

commit v3 on v2

v3 whole, which is shorter than its diff:
```python
import jax
import jax.numpy as jnp
from jax import lax
from jax.experimental import pallas as pl
from jax.experimental.pallas import tpu as pltpu
from jax.sharding import PartitionSpec as P

CAP = 8
F32 = jnp.float32
BF16 = jnp.bfloat16


def slot_mask(routes, experts):
    rows, top = routes.shape
    slots = experts * CAP
    lane = lax.broadcasted_iota(jnp.int32, (rows, slots), 1)
    owner = lane >> 3
    named = routes[:, 0:1] == owner
    for k in range(1, top):
        named = named | (routes[:, k : k + 1] == owner)
    earlier = lax.broadcasted_iota(jnp.int32, (rows, rows), 1) < lax.broadcasted_iota(
        jnp.int32, (rows, rows), 0
    )
    rank = jnp.dot(
        earlier.astype(F32).astype(BF16), named.astype(F32).astype(BF16), preferred_element_type=F32
    )
    return named & (rank == (lane & 7).astype(F32))


def pack_kernel(
    hidden_hbm, gain_hbm, routes_hbm, gates_hbm, out_ref, weights_ref, hidden, gain, routes, gates, sem
):
    copies = [
        pltpu.make_async_copy(source, held, sem.at[i])
        for i, (source, held) in enumerate(
            ((routes_hbm, routes), (gates_hbm, gates), (hidden_hbm, hidden), (gain_hbm, gain))
        )
    ]
    for copy in copies:
        copy.start()
    for copy in copies:
        copy.wait()
    steps, rows, width = hidden.shape
    experts = out_ref.shape[0]
    slots = experts * CAP
    owner = lax.broadcasted_iota(jnp.int32, (rows, slots), 1) >> 3
    for step in range(steps):
        xf = hidden[step].astype(F32)
        scale = lax.rsqrt(jnp.mean(xf * xf, axis=-1, keepdims=True) + 1e-06)
        normed = (xf * scale * gain[...]).astype(BF16)
        named_by = routes[step].T
        gate_of = gates[step].T
        mask = slot_mask(named_by, experts)
        spread = mask.astype(F32).astype(BF16)
        packed = lax.dot_general(
            spread, normed, (((0,), (0,)), ((), ())), preferred_element_type=F32
        )
        out_ref[:, step] = packed.reshape(experts, CAP, width).astype(BF16)
        weight = jnp.zeros((rows, slots), F32)
        for k in range(named_by.shape[1]):
            weight = jnp.where(named_by[:, k : k + 1] == owner, gate_of[:, k : k + 1], weight)
        weight = jnp.where(mask, weight, 0.0)
        high = weight.astype(BF16)
        rest = weight - high.astype(F32)
        mid = rest.astype(BF16)
        low = (rest - mid.astype(F32)).astype(BF16)
        weights_ref[step, 0:rows] = high
        weights_ref[step, rows : 2 * rows] = mid
        weights_ref[step, 2 * rows : 3 * rows] = low


def expert_kernel(version_ref, rows_ref, *refs):
    weights_refs, out_ref = refs[:-1], refs[-1]
    sources, _, cap, width = rows_ref.shape
    step = pl.program_id(0)
    nt = (((1,), (1,)), ((), ()))

    def matrix(i):
        return jnp.concatenate([ref[0, i] for ref in weights_refs], axis=0)

    rows_in = rows_ref[:, step].astype(F32).reshape(sources * cap, width).astype(BF16)
    gate_v = lax.dot_general(rows_in, matrix(0), nt, preferred_element_type=F32)
    up_v = lax.dot_general(rows_in, matrix(1), nt, preferred_element_type=F32)
    act = (gate_v / (1.0 + jnp.exp(-gate_v)) * up_v).astype(BF16)
    made = jnp.dot(act, matrix(2), preferred_element_type=F32)
    out_ref[:, step] = made.reshape(sources, cap, width).astype(BF16)


def combine_kernel(hidden_ref, weights_ref, back_ref, out_ref):
    steps, rows, width = hidden_ref.shape
    experts, _, cap, _ = back_ref.shape
    for step in range(steps):
        outputs = back_ref[:, step].astype(F32).reshape(experts * cap, width).astype(BF16)
        parts = jnp.dot(weights_ref[step], outputs, preferred_element_type=F32)
        total = parts[2 * rows :] + parts[rows : 2 * rows] + parts[:rows]
        out_ref[step] = (hidden_ref[step].astype(F32) + total).astype(BF16)


def local(hidden, norm_gain, routes, gates, switch, experts_old, experts_new):
    steps, rows, width = hidden.shape
    top = routes.shape[2]
    exp_dev, mats, shard, _ = experts_old.shape
    members = lax.axis_size("expert")
    groups = lax.axis_size("group")
    experts = exp_dev * members
    slots = experts * CAP
    big = pltpu.CompilerParams(vmem_limit_bytes=48 * 1024 * 1024)
    plane = groups // 2
    core = lax.axis_index("group") % 2

    def device(low, x, c):
        return (low % 2) * plane + (x % (plane // 2)) * 2 + c % 2

    def move(array, low, x, c):
        pairs = [
            (device(l, i, k), device(l + low, i + x, k + c))
            for l in range(2)
            for i in range(plane // 2)
            for k in range(2)
        ]
        return lax.ppermute(array, "group", pairs)

    bend = lambda e: (e + 1) % 4 // 2
    rings = [
        [device(low + bend(e), x, c) * members + e for e in range(members) for c in range(2)]
        for low in range(2)
        for x in range(plane // 2)
    ]

    def exchange(blocks):
        return lax.all_to_all(
            blocks, ("group", "expert"), 0, 0, axis_index_groups=rings, tiled=True
        )

    versions = jnp.stack([experts_old, experts_new])
    mine = lax.dynamic_index_in_dim(versions, core, 1, keepdims=False)
    theirs = lax.dynamic_index_in_dim(versions, 1 - core, 1, keepdims=False)
    near = [mine, move(mine, 1, 0, 0), move(theirs, 1, 0, 1), move(theirs, 0, 0, 1)]

    far = lambda array: pltpu.with_memory_space_constraint(array, pltpu.HBM)
    outgoing, weigh = pl.pallas_call(
        pack_kernel,
        in_specs=[pl.BlockSpec(memory_space=pltpu.HBM)] * 4,
        out_shape=(
            jax.ShapeDtypeStruct((experts, steps, CAP, width), BF16),
            jax.ShapeDtypeStruct((steps, 3 * rows, slots), BF16),
        ),
        scratch_shapes=[
            pltpu.VMEM(hidden.shape, BF16),
            pltpu.VMEM((1, width), F32),
            pltpu.VMEM((steps, top, rows), jnp.int32),
            pltpu.VMEM((steps, top, rows), F32),
            pltpu.SemaphoreType.DMA((4,)),
        ],
        compiler_params=big,
        cost_estimate=pl.CostEstimate(
            flops=2 * steps * rows * slots * width, bytes_accessed=4 << 20, transcendentals=0
        ),
        name="pack",
    )(
        far(hidden),
        far(norm_gain.reshape(1, width)),
        far(routes.transpose(0, 2, 1)),
        far(gates.transpose(0, 2, 1)),
    )
    near, outgoing = lax.optimization_barrier((near, outgoing))
    received = exchange(outgoing)
    block = jnp.concatenate(near, axis=2)
    blocks = [block] + [move(block, 0, x, 0) for x in (2, 1, -1)]

    own = lax.axis_index("expert") * exp_dev + core
    version = (jnp.arange(steps, dtype=jnp.int32) >= switch[own]).astype(jnp.int32)
    whole = pl.BlockSpec(memory_space=pltpu.VMEM)
    produced = pl.pallas_call(
        expert_kernel,
        grid_spec=pltpu.PrefetchScalarGridSpec(
            num_scalar_prefetch=1,
            grid=(steps,),
            in_specs=[whole]
            + [pl.BlockSpec((1,) + block.shape[1:], lambda s, v: (v[s], 0, 0, 0))] * len(blocks),
            out_specs=whole,
        ),
        out_shape=jax.ShapeDtypeStruct((experts, steps, CAP, width), BF16),
        compiler_params=big,
        name="experts",
    )(version, received, *blocks)
    returned = exchange(produced)
    return pl.pallas_call(
        combine_kernel,
        out_shape=jax.ShapeDtypeStruct((steps, rows, width), BF16),
        compiler_params=big,
        name="combine",
    )(hidden, weigh, returned)


def solution(mesh):
    in_specs = (
        P(None, ("group", "expert"), None),
        P(),
        P(None, ("group", "expert"), None),
        P(None, ("group", "expert"), None),
        P(),
        P("expert", None, "group", None),
        P("expert", None, "group", None),
    )
    out_specs = P(None, ("group", "expert"), None)
    return jax.shard_map(local, mesh=mesh, in_specs=in_specs, out_specs=out_specs, check_vma=False)
```

time: 244 us -> 210 us (0.86); the launches traced: 243 us -> 207 us
  waiting for transfers between devices: 87.3 us -> 68 us
  starting transfers between devices: 21.1 us -> 34.6 us
  between operations: 13.5 us -> 0.15 us
  blocking collectives: 98 us -> 85.4 us
  local copies, waits for them, and re-layouts: 5.02 us -> 1.38 us
    all_to_all x1, waiting for transfers between devices: 82.3 us -> 12.5 us  [exchange(): lax.all_to_all(blocks, ('group', 'expert'), 0, 0, axis_index_groups=rings...]
    ppermute x2 -> x6, waiting for transfers between devices: 4.97 us -> 55.5 us  [move(): return lax.ppermute(array, 'group', pairs)]
    ppermute x2 -> x6, starting transfers between devices: 6.19 us -> 19 us  [move(): return lax.ppermute(array, 'group', pairs)]
    all_to_all x1, blocking collectives: 98 us -> 85.4 us  [exchange(): lax.all_to_all(blocks, ('group', 'expert'), 0, 0, axis_index_groups=rings...]
    unnamed x12 -> x11, local copies, waits for them, and re-layouts: 4.85 us -> 0.78 us
  transfers between devices with their start and end apart: 4 -> 7, of which waited for: 2 -> 5; matrix products, arithmetic and copies ran while one was open for 1% -> 1% of each run, Pallas kernels for 1% -> 2%
where the time goes in v3:
time: 210 us; the launch traced here: 207 us
  blocking collectives  85.4 us (41%)
  waiting for transfers between devices  68 us (32%)
  starting transfers between devices  34.6 us (16%)
  Pallas kernels  15.5 us (7%)
    all_to_all x1, blocking collectives, exchange(): lax.all_to_all(blocks, ('group', 'expert'), 0, 0, axis_index_groups=rings...  85.4 us
    ppermute x6, waiting for transfers between devices, move(): return lax.ppermute(array, 'group', pairs)  55.5 us
    ppermute x6, starting transfers between devices, move(): return lax.ppermute(array, 'group', pairs)  19 us
    all_to_all x1, starting transfers between devices, exchange(): lax.all_to_all(blocks, ('group', 'expert'), 0, 0, axis_index_groups=rings...  15.6 us
    all_to_all x1, waiting for transfers between devices, exchange(): lax.all_to_all(blocks, ('group', 'expert'), 0, 0, axis_index_groups=rings...  12.5 us
    pallas_call x1, Pallas kernels, local(): pl.pallas_call(expert_kernel, grid_spec=pltpu.PrefetchScalarGridSpec(num_...  9.77 us
    pallas_call x1, Pallas kernels, local(): pl.pallas_call(pack_kernel, in_specs=[pl.BlockSpec(memory_space=pltpu.HBM...  4.45 us
  transfers between devices with their start and end apart: 7, of which 5 were waited for; matrix products, arithmetic and copies ran while one was open for 1% of the time, Pallas kernels for 2%

profile of v3, /device:TPU:56, one launch (start us, length us, event | category | flops | bytes accessed | tf_op | source)
XLA Modules:
  0.0 206.9 jit_solution(11942630090892987566)
XLA Ops:
  0.0 1.2 fusion.1
  1.2 1.9 collective-permute-start.2
  3.1 4.4 %collective-permute-start.1 = (bf16[2,3,24,1024]{3,2,1,0:T(8,128)(2,1)S(1)}, bf16[2,3,24,1024]{3,2,1,0:T(8,128)(2,1)S(1)}, u32[]{:S(2)}, u32[]{:S(2)}) collective-permute-start(bf16[2,3,24,1024]{3,2,1,0:T(8,128)(2,1)S(1)} %get-tuple-element.19), channel_id=1, source_target_pairs={{0,288},{32,256},{64,352},{96,320},{128,416},{160,384},{192,480},{... | collective-permute-start | bytes 884744 | tf_op jit(solution)/shard_map/ppermute | solution.py:121
  7.5 1.9 collective-permute-start
  9.4 4.5 %pack.1 = (bf16[64,3,8,1024]{3,2,1,0:T(8,128)(2,1)}, bf16[3,96,512]{2,1,0:T(8,128)(2,1)S(1)}) custom-call(bf16[3,32,1024]{2,1,0:T(8,128)(2,1)} %hidden_ref.1, f32[1,1024]{1,0:T(1,128)} %bitcast.14, s32[3,8,32]{2,1,0:T(8,128)} %bitcast.12, f32[3,8,32]{2,1,0:T(8,128)} %bitcast.13), custom_call_target="tpu_custom_call" | custom-call | flops 100663296 | bytes 4194304 | tf_op jit(solution)/shard_map/pack/pallas_call | solution.py:141
  13.9 0.0 copy-start
  13.9 0.7 copy-done
  14.6 0.0 collective-permute-done.2
  14.6 0.3 collective-permute-done.1
  14.9 6.5 %collective-permute-done = bf16[2,3,24,1024]{3,2,1,0:T(8,128)(2,1)S(1)} collective-permute-done((bf16[2,3,24,1024]{3,2,1,0:T(8,128)(2,1)S(1)}, bf16[2,3,24,1024]{3,2,1,0:T(8,128)(2,1)S(1)}, u32[]{:S(2)}, u32[]{:S(2)}) %collective-permute-start) | collective-permute-done | bytes 294944 | tf_op jit(solution)/shard_map/ppermute | solution.py:121
  21.4 15.6 %all-to-all-start = ((bf16[64,3,8,1024]{3,2,1,0:T(8,128)(2,1)}), bf16[64,3,8,1024]{3,2,1,0:T(8,128)(2,1)}, u32[]{:S(2)}, u32[]{:S(2)}) async-start(bf16[64,3,8,1024]{3,2,1,0:T(8,128)(2,1)} %get-tuple-element.14), calls=%async_computation | async-start | bytes 6291456 | tf_op jit(solution)/shard_map/all_to_all | solution.py:131
  37.0 0.0 copy-start.3
  37.1 4.7 %collective-permute-start.5 = (bf16[2,3,96,1024]{3,2,1,0:T(8,128)(2,1)S(1)}, bf16[2,3,96,1024]{3,2,1,0:T(8,128)(2,1)S(1)}, u32[]{:S(2)}, u32[]{:S(2)}) collective-permute-start(bf16[2,3,96,1024]{3,2,1,0:T(8,128)(2,1)S(1)} %constant_dynamic-update-slice_fusion.refs_0_), channel_id=1, source_target_pairs={{0,192},{32,224},{64,0},{96,32},{128,64},{160,96},{192,128},{224,1... | collective-permute-start | bytes 3538952 | tf_op jit(solution)/shard_map/ppermute | solution.py:121
  41.8 1.9 collective-permute-start.4
  43.7 4.2 %collective-permute-start.3 = (bf16[2,3,96,1024]{3,2,1,0:T(8,128)(2,1)S(1)}, bf16[2,3,96,1024]{3,2,1,0:T(8,128)(2,1)}, u32[]{:S(2)}, u32[]{:S(2)}) collective-permute-start(bf16[2,3,96,1024]{3,2,1,0:T(8,128)(2,1)S(1)} %constant_dynamic-update-slice_fusion.refs_0_), channel_id=1, source_target_pairs={{0,128},{32,160},{64,192},{96,224},{128,0},{160,32},{192,64},{224,... | collective-permute-start | bytes 3538952 | tf_op jit(solution)/shard_map/ppermute | solution.py:121
  47.9 0.6 dynamic_slice.10
  48.5 0.6 compare_convert_fusion.version_ref
  49.1 43.4 %collective-permute-done.5.refs_3_ = bf16[2,3,96,1024]{3,2,1,0:T(8,128)(2,1)S(1)} collective-permute-done((bf16[2,3,96,1024]{3,2,1,0:T(8,128)(2,1)S(1)}, bf16[2,3,96,1024]{3,2,1,0:T(8,128)(2,1)S(1)}, u32[]{:S(2)}, u32[]{:S(2)}) %collective-permute-start.5) | collective-permute-done | bytes 1179680 | tf_op jit(solution)/shard_map/ppermute | solution.py:121
  92.6 5.3 %collective-permute-done.4.refs_2_ = bf16[2,3,96,1024]{3,2,1,0:T(8,128)(2,1)S(1)} collective-permute-done((bf16[2,3,96,1024]{3,2,1,0:T(8,128)(2,1)S(1)}, bf16[2,3,96,1024]{3,2,1,0:T(8,128)(2,1)S(1)}, u32[]{:S(2)}, u32[]{:S(2)}) %collective-permute-start.4) | collective-permute-done | bytes 1179680 | tf_op jit(solution)/shard_map/ppermute | solution.py:121
  97.9 0.0 collective-permute-done.3.refs_1_
  97.9 12.5 %all-to-all-done.rows_ref = bf16[64,3,8,1024]{3,2,1,0:T(8,128)(2,1)} async-done(((bf16[64,3,8,1024]{3,2,1,0:T(8,128)(2,1)}), bf16[64,3,8,1024]{3,2,1,0:T(8,128)(2,1)}, u32[]{:S(2)}, u32[]{:S(2)}) %all-to-all-start) | async-done | bytes 3145760 | tf_op jit(solution)/shard_map/all_to_all | solution.py:131
  110.3 9.8 %experts.1 = bf16[64,3,8,1024]{3,2,1,0:T(8,128)(2,1)} custom-call(s32[3]{0:T(128)S(1)} %compare_convert_fusion.version_ref, bf16[64,3,8,1024]{3,2,1,0:T(8,128)(2,1)} %all-to-all-done.rows_ref, bf16[2,3,96,1024]{3,2,1,0:T(8,128)(2,1)S(1)} %constant_dynamic-update-slice_fusion.refs_0_, bf16[2,3,96,1024]{3,2,1,0:T(8,128)(2,1)} %collective-permute-done.3.refs_1_, ...), custom_call_target="tpu_custom_call" | custom-call | tf_op jit(solution)/shard_map/experts/pallas_call | solution.py:174
  120.1 85.4 %all_to_all.10.back_ref = bf16[64,3,8,1024]{3,2,1,0:T(8,128)(2,1)S(1)} all-to-all(bf16[64,3,8,1024]{3,2,1,0:T(8,128)(2,1)} %experts.1), channel_id=1, replica_groups={{0,32,257,289,258,290,3,35,4,36,261,293,262,294,7,39,8,40,265,297,266,2..., dimensions={0} | all-to-all | bytes 6291456 | tf_op jit(solution)/shard_map/all_to_all | solution.py:131
  205.5 1.3 combine.1
  (9 shorter events, 0.1 us)
Async XLA Ops:
  1.2 13.4 %collective-permute-start.2 = (bf16[2,3,24,1024]{3,2,1,0:T(8,128)(2,1)S(1)}, bf16[2,3,24,1024]{3,2,1,0:T(8,128)(2,1)S(1)}, u32[]{:S(2)}, u32[]{:S(2)}) collective-permute-start(bf16[2,3,24,1024]{3,2,1,0:T(8,128)(2,1)S(1)} %get-tuple-element.19), channel_id=1, source_target_pairs={{0,32},{32,0},{64,96},{96,64},{128,160},{160,128},{192,224},{224,1... | collective-permute-start | bytes 884744 | tf_op jit(solution)/shard_map/ppermute | solution.py:121
  3.1 11.7 %collective-permute-start.1 = (bf16[2,3,24,1024]{3,2,1,0:T(8,128)(2,1)S(1)}, bf16[2,3,24,1024]{3,2,1,0:T(8,128)(2,1)S(1)}, u32[]{:S(2)}, u32[]{:S(2)}) collective-permute-start(bf16[2,3,24,1024]{3,2,1,0:T(8,128)(2,1)S(1)} %get-tuple-element.19), channel_id=1, source_target_pairs={{0,288},{32,256},{64,352},{96,320},{128,416},{160,384},{192,480},{... | collective-permute-start | bytes 884744 | tf_op jit(solution)/shard_map/ppermute | solution.py:121
  7.5 13.9 %collective-permute-start = (bf16[2,3,24,1024]{3,2,1,0:T(8,128)(2,1)S(1)}, bf16[2,3,24,1024]{3,2,1,0:T(8,128)(2,1)S(1)}, u32[]{:S(2)}, u32[]{:S(2)}) collective-permute-start(bf16[2,3,24,1024]{3,2,1,0:T(8,128)(2,1)S(1)} %get-tuple-element.15), channel_id=1, source_target_pairs={{0,256},{32,288},{64,320},{96,352},{128,384},{160,416},{192,448},{... | collective-permute-start | bytes 884744 | tf_op jit(solution)/shard_map/ppermute | solution.py:121
  13.9 0.7 copy-start
  21.4 89.0 %all-to-all-start = ((bf16[64,3,8,1024]{3,2,1,0:T(8,128)(2,1)}), bf16[64,3,8,1024]{3,2,1,0:T(8,128)(2,1)}, u32[]{:S(2)}, u32[]{:S(2)}) async-start(bf16[64,3,8,1024]{3,2,1,0:T(8,128)(2,1)} %get-tuple-element.14), calls=%async_computation | async-start | bytes 6291456 | tf_op jit(solution)/shard_map/all_to_all | solution.py:131
  37.0 10.9 %copy-start.3 = (s32[64]{0:T(128)S(1)}, s32[64]{0:T(128)}, u32[]{:S(2)}) copy-start(s32[64]{0:T(128)} %param.11) | copy-start | bytes 772
  37.1 55.5 %collective-permute-start.5 = (bf16[2,3,96,1024]{3,2,1,0:T(8,128)(2,1)S(1)}, bf16[2,3,96,1024]{3,2,1,0:T(8,128)(2,1)S(1)}, u32[]{:S(2)}, u32[]{:S(2)}) collective-permute-start(bf16[2,3,96,1024]{3,2,1,0:T(8,128)(2,1)S(1)} %constant_dynamic-update-slice_fusion.refs_0_), channel_id=1, source_target_pairs={{0,192},{32,224},{64,0},{96,32},{128,64},{160,96},{192,128},{224,1... | collective-permute-start | bytes 3538952 | tf_op jit(solution)/shard_map/ppermute | solution.py:121
  41.8 56.1 %collective-permute-start.4 = (bf16[2,3,96,1024]{3,2,1,0:T(8,128)(2,1)S(1)}, bf16[2,3,96,1024]{3,2,1,0:T(8,128)(2,1)S(1)}, u32[]{:S(2)}, u32[]{:S(2)}) collective-permute-start(bf16[2,3,96,1024]{3,2,1,0:T(8,128)(2,1)S(1)} %constant_dynamic-update-slice_fusion.refs_0_), channel_id=1, source_target_pairs={{0,64},{32,96},{64,128},{96,160},{128,192},{160,224},{192,0},{224,... | collective-permute-start | bytes 3538952 | tf_op jit(solution)/shard_map/ppermute | solution.py:121
  43.7 54.2 %collective-permute-start.3 = (bf16[2,3,96,1024]{3,2,1,0:T(8,128)(2,1)S(1)}, bf16[2,3,96,1024]{3,2,1,0:T(8,128)(2,1)}, u32[]{:S(2)}, u32[]{:S(2)}) collective-permute-start(bf16[2,3,96,1024]{3,2,1,0:T(8,128)(2,1)S(1)} %constant_dynamic-update-slice_fusion.refs_0_), channel_id=1, source_target_pairs={{0,128},{32,160},{64,192},{96,224},{128,0},{160,32},{192,64},{224,... | collective-permute-start | bytes 3538952 | tf_op jit(solution)/shard_map/ppermute | solution.py:121
  120.1 85.4 %copy-start.1 = (bf16[3,96,512]{2,1,0:T(8,128)(2,1)S(1)}, bf16[3,96,512]{2,1,0:T(8,128)(2,1)}, u32[]{:S(2)}) copy-start(bf16[3,96,512]{2,1,0:T(8,128)(2,1)} %copy-done) | copy-start | bytes 884740
  120.1 85.4 %copy-start.2 = (bf16[3,32,1024]{2,1,0:T(8,128)(2,1)S(1)}, bf16[3,32,1024]{2,1,0:T(8,128)(2,1)}, u32[]{:S(2)}) copy-start(bf16[3,32,1024]{2,1,0:T(8,128)(2,1)} %hidden_ref.1) | copy-start | bytes 589828

commit v4 on v3

v4 whole, which is shorter than its diff:
```python
import jax
import jax.numpy as jnp
from jax import lax
from jax.experimental import pallas as pl
from jax.experimental.pallas import tpu as pltpu
from jax.sharding import PartitionSpec as P

CAP = 8
F32 = jnp.float32
BF16 = jnp.bfloat16


def slot_mask(routes, experts):
    rows, top = routes.shape
    slots = experts * CAP
    lane = lax.broadcasted_iota(jnp.int32, (rows, slots), 1)
    owner = lane >> 3
    named = routes[:, 0:1] == owner
    for k in range(1, top):
        named = named | (routes[:, k : k + 1] == owner)
    earlier = lax.broadcasted_iota(jnp.int32, (rows, rows), 1) < lax.broadcasted_iota(
        jnp.int32, (rows, rows), 0
    )
    rank = jnp.dot(
        earlier.astype(F32).astype(BF16), named.astype(F32).astype(BF16), preferred_element_type=F32
    )
    return named & (rank == (lane & 7).astype(F32))


def pack_kernel(
    hidden_hbm, gain_hbm, routes_hbm, out_hbm, hidden, gain, routes, packed, in_sem, out_sem
):
    copies = [
        pltpu.make_async_copy(source, held, in_sem.at[i])
        for i, (source, held) in enumerate(
            ((routes_hbm, routes), (hidden_hbm, hidden), (gain_hbm, gain))
        )
    ]
    for copy in copies:
        copy.start()
    for copy in copies:
        copy.wait()
    steps, experts, cap, width = packed.shape
    leaving = []
    for step in range(steps):
        xf = hidden[step].astype(F32)
        scale = lax.rsqrt(jnp.mean(xf * xf, axis=-1, keepdims=True) + 1e-06)
        normed = (xf * scale * gain[...]).astype(BF16)
        spread = slot_mask(routes[step].T, experts).astype(F32).astype(BF16)
        rows_out = lax.dot_general(
            spread, normed, (((0,), (0,)), ((), ())), preferred_element_type=F32
        )
        packed[step] = rows_out.reshape(experts, cap, width).astype(BF16)
        leaving.append(
            pltpu.make_async_copy(packed.at[step], out_hbm.at[:, step], out_sem.at[step])
        )
        leaving[-1].start()
    for copy in leaving:
        copy.wait()


def weigh_kernel(routes_ref, gates_ref, out_ref):
    steps, top, rows = routes_ref.shape
    slots = out_ref.shape[2]
    owner = lax.broadcasted_iota(jnp.int32, (rows, slots), 1) >> 3
    for step in range(steps):
        named_by = routes_ref[step].T
        gate_of = gates_ref[step].T
        mask = slot_mask(named_by, slots // CAP)
        weight = jnp.zeros((rows, slots), F32)
        for k in range(top):
            weight = jnp.where(named_by[:, k : k + 1] == owner, gate_of[:, k : k + 1], weight)
        weight = jnp.where(mask, weight, 0.0)
        high = weight.astype(BF16)
        rest = weight - high.astype(F32)
        mid = rest.astype(BF16)
        low = (rest - mid.astype(F32)).astype(BF16)
        out_ref[step, 0:rows] = high
        out_ref[step, rows : 2 * rows] = mid
        out_ref[step, 2 * rows : 3 * rows] = low


def sort_kernel(core_ref, *refs):
    sources, (mine_ref, theirs_ref) = refs[:-2], refs[-2:]
    core = core_ref[0]
    shard = sources[0].shape[2]
    for i, source in enumerate(sources):
        place = pl.ds(i // 2 * shard, shard)
        mine_ref[i % 2, :, place] = source[core]
        theirs_ref[i % 2, :, place] = source[1 - core]


def join_kernel(*refs):
    parts, out_ref = refs[:-1], refs[-1]
    shard = parts[0].shape[2]
    for i, part in enumerate(parts):
        out_ref[:, :, i * shard : (i + 1) * shard] = part[...]


def expert_kernel(switch_ref, own_ref, rows_ref, *refs):
    blocks, (out_ref, weights, sem) = refs[:-3], refs[-3:]
    sources, steps, cap, width = rows_ref.shape
    mats, part = blocks[0].shape[1:3]
    first_new = switch_ref[own_ref[0]]
    version_at = lambda step: (step >= first_new).astype(jnp.int32)
    nt = (((1,), (1,)), ((), ()))

    def copies(version, i):
        return [
            pltpu.make_async_copy(
                block.at[version, i],
                weights.at[version, i, pl.ds(b * part, part)],
                sem.at[version, i, b],
            )
            for b, block in enumerate(blocks)
        ]

    def fetch(version):
        for i in range(mats):
            for copy in copies(version, i):
                copy.start()

    def arrive(version, i):
        for copy in copies(version, i):
            copy.wait()

    both = (first_new > 0) & (first_new < steps)
    fetch(version_at(0))
    pl.when(both)(lambda: fetch(1))
    for step in range(steps):
        version = version_at(step)
        if step == 0:
            arrive(version, 0)
        else:

            @pl.when(first_new == step)
            def _():
                for i in range(mats):
                    arrive(1, i)

        rows_in = rows_ref[:, step].astype(F32).reshape(sources * cap, width).astype(BF16)
        gate_v = lax.dot_general(rows_in, weights[version, 0], nt, preferred_element_type=F32)
        if step == 0:
            arrive(version, 1)
        up_v = lax.dot_general(rows_in, weights[version, 1], nt, preferred_element_type=F32)
        act = (gate_v / (1.0 + jnp.exp(-gate_v)) * up_v).astype(BF16)
        if step == 0:
            arrive(version, 2)
        made = jnp.dot(act, weights[version, 2], preferred_element_type=F32)
        out_ref[:, step] = made.reshape(sources, cap, width).astype(BF16)


def combine_kernel(hidden_ref, weights_ref, back_ref, out_ref):
    steps, rows, width = hidden_ref.shape
    experts, _, cap, _ = back_ref.shape
    for step in range(steps):
        outputs = back_ref[:, step].astype(F32).reshape(experts * cap, width).astype(BF16)
        parts = jnp.dot(weights_ref[step], outputs, preferred_element_type=F32)
        total = parts[2 * rows :] + parts[rows : 2 * rows] + parts[:rows]
        out_ref[step] = (hidden_ref[step].astype(F32) + total).astype(BF16)


def local(hidden, norm_gain, routes, gates, switch, experts_old, experts_new):
    steps, rows, width = hidden.shape
    top = routes.shape[2]
    exp_dev, mats, shard, _ = experts_old.shape
    members = lax.axis_size("expert")
    groups = lax.axis_size("group")
    experts = exp_dev * members
    slots = experts * CAP
    limit = lambda mib: pltpu.CompilerParams(vmem_limit_bytes=mib * 1024 * 1024)
    plane = groups // 2
    core = lax.axis_index("group") % 2

    def device(low, x, c):
        return (low % 2) * plane + (x % (plane // 2)) * 2 + c % 2

    def move(array, low, x, c):
        pairs = [
            (device(l, i, k), device(l + low, i + x, k + c))
            for l in range(2)
            for i in range(plane // 2)
            for k in range(2)
        ]
        return lax.ppermute(array, "group", pairs)

    bend = lambda e: (e + 1) % 4 // 2
    rings = [
        [device(low + bend(e), x, c) * members + e for e in range(members) for c in range(2)]
        for low in range(2)
        for x in range(plane // 2)
    ]

    def exchange(blocks):
        return lax.all_to_all(
            blocks, ("group", "expert"), 0, 0, axis_index_groups=rings, tiled=True
        )

    partner = [move(array, 1, 0, 0) for array in (experts_old, experts_new)]

    far = lambda array: pltpu.with_memory_space_constraint(array, pltpu.HBM)
    routes = routes.transpose(0, 2, 1)
    gates = gates.transpose(0, 2, 1)
    outgoing = pl.pallas_call(
        pack_kernel,
        in_specs=[pl.BlockSpec(memory_space=pltpu.HBM)] * 3,
        out_specs=pl.BlockSpec(memory_space=pltpu.HBM),
        out_shape=pltpu.HBM((experts, steps, CAP, width), BF16),
        scratch_shapes=[
            pltpu.VMEM(hidden.shape, BF16),
            pltpu.VMEM((1, width), F32),
            pltpu.VMEM((steps, top, rows), jnp.int32),
            pltpu.VMEM((steps, experts, CAP, width), BF16),
            pltpu.SemaphoreType.DMA((3,)),
            pltpu.SemaphoreType.DMA((steps,)),
        ],
        compiler_params=limit(16),
        cost_estimate=pl.CostEstimate(
            flops=2 * steps * rows * slots * width, bytes_accessed=4 << 20, transcendentals=0
        ),
        name="pack",
    )(far(hidden), far(norm_gain.reshape(1, width)), far(routes))
    weigh = pl.pallas_call(
        weigh_kernel,
        out_shape=jax.ShapeDtypeStruct((steps, 3 * rows, slots), BF16),
        compiler_params=limit(16),
        name="weigh",
    )(routes, gates)
    received = exchange(outgoing)
    near = (2, mats, 2 * shard, width)
    whole = pl.BlockSpec(memory_space=pltpu.VMEM)
    mine, theirs = pl.pallas_call(
        sort_kernel,
        in_specs=[pl.BlockSpec(memory_space=pltpu.SMEM)] + [whole] * 4,
        out_shape=(jax.ShapeDtypeStruct(near, BF16), jax.ShapeDtypeStruct(near, BF16)),
        compiler_params=limit(16),
        cost_estimate=pl.CostEstimate(flops=100_000_000_000, bytes_accessed=4 << 20, transcendentals=0),
        name="sort",
    )(core.reshape(1), experts_old, experts_new, *partner)
    block = pl.pallas_call(
        join_kernel,
        out_shape=jax.ShapeDtypeStruct((2, mats, 4 * shard, width), BF16),
        compiler_params=limit(16),
        name="join",
    )(mine, move(theirs, 0, 0, 1))
    blocks = [block] + [move(block, 0, x, 0) for x in (2, 1, -1)]

    received, weigh = lax.optimization_barrier((received, weigh))
    own = lax.axis_index("expert") * exp_dev + core
    produced = pl.pallas_call(
        expert_kernel,
        grid_spec=pltpu.PrefetchScalarGridSpec(
            num_scalar_prefetch=2,
            grid=(1,),
            in_specs=[whole] + [pl.BlockSpec(memory_space=pltpu.HBM)] * len(blocks),
            out_specs=whole,
            scratch_shapes=[
                pltpu.VMEM((2, mats, shard * groups, width), BF16),
                pltpu.SemaphoreType.DMA((2, mats, len(blocks))),
            ],
        ),
        out_shape=jax.ShapeDtypeStruct((experts, steps, CAP, width), BF16),
        compiler_params=limit(28),
        name="experts",
    )(switch, own.reshape(1), received, *(far(part) for part in blocks))
    returned = exchange(produced)
    return pl.pallas_call(
        combine_kernel,
        out_shape=jax.ShapeDtypeStruct((steps, rows, width), BF16),
        compiler_params=limit(16),
        name="combine",
    )(hidden, weigh, returned)


def solution(mesh):
    in_specs = (
        P(None, ("group", "expert"), None),
        P(),
        P(None, ("group", "expert"), None),
        P(None, ("group", "expert"), None),
        P(),
        P("expert", None, "group", None),
        P("expert", None, "group", None),
    )
    out_specs = P(None, ("group", "expert"), None)
    return jax.shard_map(local, mesh=mesh, in_specs=in_specs, out_specs=out_specs, check_vma=False)
```

time: 210 us -> 197 us (0.938)
  waiting for transfers between devices: 68 us -> 55.3 us
    ppermute x6, waiting for transfers between devices: 55.5 us -> 1.85 us  [move(): return lax.ppermute(array, 'group', pairs)]
    all_to_all x1, waiting for transfers between devices: 12.5 us -> 53.5 us  [exchange(): lax.all_to_all(blocks, ('group', 'expert'), 0, 0, axis_index_groups=rings...]
    pallas_call x0 -> x3, Pallas kernels: none -> 2.87 us  [the longest x1 1.17 us: local(): pl.pallas_call(sort_kernel, in_specs=[pl.BlockSpec(memory_space=pltpu.SME...]
  transfers between devices with their start and end apart: 7 -> 7, of which waited for: 5 -> 2; matrix products, arithmetic and copies ran while one was open for 1% -> 0% of each run, Pallas kernels for 2% -> 3%
where the time goes in v4:
time: 197 us; the launch traced here: 194 us
  blocking collectives  85.1 us (43%)
  waiting for transfers between devices  55.3 us (28%)
  starting transfers between devices  36.2 us (18%)
  Pallas kernels  15.8 us (8%)
    all_to_all x1, blocking collectives, exchange(): lax.all_to_all(blocks, ('group', 'expert'), 0, 0, axis_index_groups=rings...  85.1 us
    all_to_all x1, waiting for transfers between devices, exchange(): lax.all_to_all(blocks, ('group', 'expert'), 0, 0, axis_index_groups=rings...  53.5 us
    ppermute x6, starting transfers between devices, move(): return lax.ppermute(array, 'group', pairs)  20.2 us
    all_to_all x1, starting transfers between devices, exchange(): lax.all_to_all(blocks, ('group', 'expert'), 0, 0, axis_index_groups=rings...  15.9 us
    pallas_call x1, Pallas kernels, local(): pl.pallas_call(expert_kernel, grid_spec=pltpu.PrefetchScalarGridSpec(num_...  7.85 us
  transfers between devices with their start and end apart: 7, of which 2 were waited for; matrix products, arithmetic and copies ran while one was open for 0% of the time, Pallas kernels for 3%

profile of v4, /device:TPU:56, one launch (start us, length us, event | category | flops | bytes accessed | tf_op | source)
XLA Modules:
  0.0 193.6 jit_solution(11897455961808012886)
XLA Ops:
  0.0 4.3 %collective-permute-start = (bf16[2,3,24,1024]{3,2,1,0:T(8,128)(2,1)}, bf16[2,3,24,1024]{3,2,1,0:T(8,128)(2,1)}, u32[]{:S(2)}, u32[]{:S(2)}) collective-permute-start(bf16[2,3,24,1024]{3,2,1,0:T(8,128)(2,1)} %refs_0_.1), channel_id=1, source_target_pairs={{0,256},{32,288},{64,320},{96,352},{128,384},{160,416},{192,448},{... | collective-permute-start | bytes 884744 | tf_op jit(solution)/shard_map/ppermute | solution.py:185
  4.3 1.9 collective-permute-start.1
  6.2 3.8 %pack.1 = bf16[64,3,8,1024]{3,2,1,0:T(8,128)(2,1)} custom-call(bf16[3,32,1024]{2,1,0:T(8,128)(2,1)} %hidden_ref.1, f32[1,1024]{1,0:T(1,128)} %bitcast.8, s32[3,8,32]{2,1,0:T(8,128)} %bitcast.5), custom_call_target="tpu_custom_call" | custom-call | flops 100663296 | bytes 4194304 | tf_op jit(solution)/shard_map/pack/pallas_call | solution.py:204
  10.0 0.0 copy-start.4
  10.0 15.9 %all-to-all-start = ((bf16[64,3,8,1024]{3,2,1,0:T(8,128)(2,1)}), bf16[64,3,8,1024]{3,2,1,0:T(8,128)(2,1)S(1)}, u32[]{:S(2)}, u32[]{:S(2)}) async-start(bf16[64,3,8,1024]{3,2,1,0:T(8,128)(2,1)} %pack.1), calls=%async_computation | async-start | bytes 6291456 | tf_op jit(solution)/shard_map/all_to_all | solution.py:195
  26.0 0.0 collective-permute-done.refs_2_
  26.0 0.0 collective-permute-done.1.refs_3_
  26.0 0.0 copy-start.5
  26.0 1.0 copy-done.5
  27.0 1.2 sort.1
  28.1 2.1 %collective-permute-start.2 = (bf16[2,3,48,1024]{3,2,1,0:T(8,128)(2,1)S(1)}, bf16[2,3,48,1024]{3,2,1,0:T(8,128)(2,1)S(1)}, u32[]{:S(2)}, u32[]{:S(2)}) collective-permute-start(bf16[2,3,48,1024]{3,2,1,0:T(8,128)(2,1)S(1)} %get-tuple-element.12), channel_id=1, source_target_pairs={{0,32},{32,0},{64,96},{96,64},{128,160},{160,128},{192,224},{224,1... | collective-permute-start | bytes 1769480 | tf_op jit(solution)/shard_map/ppermute | solution.py:185
  30.2 1.8 collective-permute-done.2.refs_1_
  32.0 1.1 join.1.refs_0_
  33.1 4.9 %collective-permute-start.3 = (bf16[2,3,96,1024]{3,2,1,0:T(8,128)(2,1)}, bf16[2,3,96,1024]{3,2,1,0:T(8,128)(2,1)}, u32[]{:S(2)}, u32[]{:S(2)}) collective-permute-start(bf16[2,3,96,1024]{3,2,1,0:T(8,128)(2,1)} %join.1.refs_0_), channel_id=1, source_target_pairs={{0,128},{32,160},{64,192},{96,224},{128,0},{160,32},{192,64},{224,... | collective-permute-start | bytes 3538952 | tf_op jit(solution)/shard_map/ppermute | solution.py:185
  38.1 2.5 %collective-permute-start.4 = (bf16[2,3,96,1024]{3,2,1,0:T(8,128)(2,1)}, bf16[2,3,96,1024]{3,2,1,0:T(8,128)(2,1)}, u32[]{:S(2)}, u32[]{:S(2)}) collective-permute-start(bf16[2,3,96,1024]{3,2,1,0:T(8,128)(2,1)} %join.1.refs_0_), channel_id=1, source_target_pairs={{0,64},{32,96},{64,128},{96,160},{128,192},{160,224},{192,0},{224,... | collective-permute-start | bytes 3538952 | tf_op jit(solution)/shard_map/ppermute | solution.py:185
  40.6 4.6 %collective-permute-start.5 = (bf16[2,3,96,1024]{3,2,1,0:T(8,128)(2,1)}, bf16[2,3,96,1024]{3,2,1,0:T(8,128)(2,1)}, u32[]{:S(2)}, u32[]{:S(2)}) collective-permute-start(bf16[2,3,96,1024]{3,2,1,0:T(8,128)(2,1)} %join.1.refs_0_), channel_id=1, source_target_pairs={{0,192},{32,224},{64,0},{96,32},{128,64},{160,96},{192,128},{224,1... | collective-permute-start | bytes 3538952 | tf_op jit(solution)/shard_map/ppermute | solution.py:185
  45.2 0.6 weigh.1.weights_ref
  45.8 53.5 %all-to-all-done.rows_ref = bf16[64,3,8,1024]{3,2,1,0:T(8,128)(2,1)S(1)} async-done(((bf16[64,3,8,1024]{3,2,1,0:T(8,128)(2,1)}), bf16[64,3,8,1024]{3,2,1,0:T(8,128)(2,1)S(1)}, u32[]{:S(2)}, u32[]{:S(2)}) %all-to-all-start) | async-done | bytes 3145760 | tf_op jit(solution)/shard_map/all_to_all | solution.py:195
  99.3 0.0 collective-permute-done.4.refs_2_
  99.3 0.0 collective-permute-done.5.refs_3_
  99.3 7.8 %experts.1 = bf16[64,3,8,1024]{3,2,1,0:T(8,128)(2,1)S(1)} custom-call(s32[64]{0:T(128)S(1)} %copy-done.3, s32[1]{0:T(128)} %bitcast.3.own_ref, bf16[64,3,8,1024]{3,2,1,0:T(8,128)(2,1)S(1)} %all-to-all-done.rows_ref, bf16[2,3,96,1024]{3,2,1,0:T(8,128)(2,1)} %join.1.refs_0_, bf16[2,3,96,1024]{3,2,1,0:T(8,128)(2,1)} %collective-permute-done.3.refs_1_, ...), custom_call_target="tpu_custom_call" | custom-call | tf_op jit(solution)/shard_map/experts/pallas_call | solution.py:250
  107.1 0.0 copy-start
  107.1 85.1 %all_to_all.10.back_ref = bf16[64,3,8,1024]{3,2,1,0:T(8,128)(2,1)S(1)} all-to-all(bf16[64,3,8,1024]{3,2,1,0:T(8,128)(2,1)S(1)} %experts.1), channel_id=1, replica_groups={{0,32,257,289,258,290,3,35,4,36,261,293,262,294,7,39,8,40,265,297,266,2..., dimensions={0} | all-to-all | bytes 6291456 | tf_op jit(solution)/shard_map/all_to_all | solution.py:195
  192.3 1.3 combine.1
  (9 shorter events, 0.0 us)
Async XLA Ops:
  0.0 26.0 %collective-permute-start = (bf16[2,3,24,1024]{3,2,1,0:T(8,128)(2,1)}, bf16[2,3,24,1024]{3,2,1,0:T(8,128)(2,1)}, u32[]{:S(2)}, u32[]{:S(2)}) collective-permute-start(bf16[2,3,24,1024]{3,2,1,0:T(8,128)(2,1)} %refs_0_.1), channel_id=1, source_target_pairs={{0,256},{32,288},{64,320},{96,352},{128,384},{160,416},{192,448},{... | collective-permute-start | bytes 884744 | tf_op jit(solution)/shard_map/ppermute | solution.py:185
  4.3 21.7 %collective-permute-start.1 = (bf16[2,3,24,1024]{3,2,1,0:T(8,128)(2,1)}, bf16[2,3,24,1024]{3,2,1,0:T(8,128)(2,1)}, u32[]{:S(2)}, u32[]{:S(2)}) collective-permute-start(bf16[2,3,24,1024]{3,2,1,0:T(8,128)(2,1)} %refs_1_.1), channel_id=1, source_target_pairs={{0,256},{32,288},{64,320},{96,352},{128,384},{160,416},{192,448},{... | collective-permute-start | bytes 884744 | tf_op jit(solution)/shard_map/ppermute | solution.py:185
  10.0 16.0 %copy-start.4 = (bf16[2,3,24,1024]{3,2,1,0:T(8,128)(2,1)S(1)}, bf16[2,3,24,1024]{3,2,1,0:T(8,128)(2,1)}, u32[]{:S(2)}) copy-start(bf16[2,3,24,1024]{3,2,1,0:T(8,128)(2,1)} %refs_0_.1) | copy-start | bytes 884740
  10.0 89.2 %all-to-all-start = ((bf16[64,3,8,1024]{3,2,1,0:T(8,128)(2,1)}), bf16[64,3,8,1024]{3,2,1,0:T(8,128)(2,1)S(1)}, u32[]{:S(2)}, u32[]{:S(2)}) async-start(bf16[64,3,8,1024]{3,2,1,0:T(8,128)(2,1)} %pack.1), calls=%async_computation | async-start | bytes 6291456 | tf_op jit(solution)/shard_map/all_to_all | solution.py:195
  26.0 1.0 copy-start.5
  27.0 18.2 %copy-start.1 = (s32[3,32,8]{1,2,0:T(8,128)S(1)}, s32[3,32,8]{1,2,0:T(8,128)}, u32[]{:S(2)}) copy-start(s32[3,32,8]{1,2,0:T(8,128)} %param.9) | copy-start | bytes 9220
  27.0 18.2 %copy-start.2 = (f32[3,32,8]{1,2,0:T(8,128)S(1)}, f32[3,32,8]{1,2,0:T(8,128)}, u32[]{:S(2)}) copy-start(f32[3,32,8]{1,2,0:T(8,128)} %param.10) | copy-start | bytes 9220
  27.0 72.3 %copy-start.3 = (s32[64]{0:T(128)S(1)}, s32[64]{0:T(128)}, u32[]{:S(2)}) copy-start(s32[64]{0:T(128)} %switch_ref.1) | copy-start | bytes 772
  28.1 3.9 %collective-permute-start.2 = (bf16[2,3,48,1024]{3,2,1,0:T(8,128)(2,1)S(1)}, bf16[2,3,48,1024]{3,2,1,0:T(8,128)(2,1)S(1)}, u32[]{:S(2)}, u32[]{:S(2)}) collective-permute-start(bf16[2,3,48,1024]{3,2,1,0:T(8,128)(2,1)S(1)} %get-tuple-element.12), channel_id=1, source_target_pairs={{0,32},{32,0},{64,96},{96,64},{128,160},{160,128},{192,224},{224,1... | collective-permute-start | bytes 1769480 | tf_op jit(solution)/shard_map/ppermute | solution.py:185
  33.1 66.1 %collective-permute-start.3 = (bf16[2,3,96,1024]{3,2,1,0:T(8,128)(2,1)}, bf16[2,3,96,1024]{3,2,1,0:T(8,128)(2,1)}, u32[]{:S(2)}, u32[]{:S(2)}) collective-permute-start(bf16[2,3,96,1024]{3,2,1,0:T(8,128)(2,1)} %join.1.refs_0_), channel_id=1, source_target_pairs={{0,128},{32,160},{64,192},{96,224},{128,0},{160,32},{192,64},{224,... | collective-permute-start | bytes 3538952 | tf_op jit(solution)/shard_map/ppermute | solution.py:185
  38.1 61.2 %collective-permute-start.4 = (bf16[2,3,96,1024]{3,2,1,0:T(8,128)(2,1)}, bf16[2,3,96,1024]{3,2,1,0:T(8,128)(2,1)}, u32[]{:S(2)}, u32[]{:S(2)}) collective-permute-start(bf16[2,3,96,1024]{3,2,1,0:T(8,128)(2,1)} %join.1.refs_0_), channel_id=1, source_target_pairs={{0,64},{32,96},{64,128},{96,160},{128,192},{160,224},{192,0},{224,... | collective-permute-start | bytes 3538952 | tf_op jit(solution)/shard_map/ppermute | solution.py:185
  40.6 58.7 %collective-permute-start.5 = (bf16[2,3,96,1024]{3,2,1,0:T(8,128)(2,1)}, bf16[2,3,96,1024]{3,2,1,0:T(8,128)(2,1)}, u32[]{:S(2)}, u32[]{:S(2)}) collective-permute-start(bf16[2,3,96,1024]{3,2,1,0:T(8,128)(2,1)} %join.1.refs_0_), channel_id=1, source_target_pairs={{0,192},{32,224},{64,0},{96,32},{128,64},{160,96},{192,128},{224,1... | collective-permute-start | bytes 3538952 | tf_op jit(solution)/shard_map/ppermute | solution.py:185
  107.1 85.1 %copy-start = (bf16[3,32,1024]{2,1,0:T(8,128)(2,1)S(1)}, bf16[3,32,1024]{2,1,0:T(8,128)(2,1)}, u32[]{:S(2)}) copy-start(bf16[3,32,1024]{2,1,0:T(8,128)(2,1)} %hidden_ref.1) | copy-start | bytes 589828

commit v5 on v4

--- a/solution.py
+++ b/solution.py
@@ -27,19 +27,24 @@
     return named & (rank == (lane & 7).astype(F32))
 
 
-def pack_kernel(
-    hidden_hbm, gain_hbm, routes_hbm, out_hbm, hidden, gain, routes, packed, in_sem, out_sem
-):
+def load_kernel(old_hbm, new_hbm, hidden_hbm, gain_hbm, routes_hbm, both, hidden, gain, routes, sem):
+    moves = (
+        (old_hbm, both.at[0]),
+        (new_hbm, both.at[1]),
+        (hidden_hbm, hidden),
+        (gain_hbm, gain),
+        (routes_hbm, routes),
+    )
     copies = [
-        pltpu.make_async_copy(source, held, in_sem.at[i])
-        for i, (source, held) in enumerate(
-            ((routes_hbm, routes), (hidden_hbm, hidden), (gain_hbm, gain))
-        )
+        pltpu.make_async_copy(source, held, sem.at[i]) for i, (source, held) in enumerate(moves)
     ]
     for copy in copies:
         copy.start()
     for copy in copies:
         copy.wait()
+
+
+def pack_kernel(hidden, gain, routes, out_hbm, packed, sem):
     steps, experts, cap, width = packed.shape
     leaving = []
     for step in range(steps):
@@ -51,9 +56,7 @@
             spread, normed, (((0,), (0,)), ((), ())), preferred_element_type=F32
         )
         packed[step] = rows_out.reshape(experts, cap, width).astype(BF16)
-        leaving.append(
-            pltpu.make_async_copy(packed.at[step], out_hbm.at[:, step], out_sem.at[step])
-        )
+        leaving.append(pltpu.make_async_copy(packed.at[step], out_hbm.at[:, step], sem.at[step]))
         leaving[-1].start()
     for copy in leaving:
         copy.wait()
@@ -83,11 +86,11 @@
 def sort_kernel(core_ref, *refs):
     sources, (mine_ref, theirs_ref) = refs[:-2], refs[-2:]
     core = core_ref[0]
-    shard = sources[0].shape[2]
+    shard = sources[0].shape[3]
     for i, source in enumerate(sources):
-        place = pl.ds(i // 2 * shard, shard)
-        mine_ref[i % 2, :, place] = source[core]
-        theirs_ref[i % 2, :, place] = source[1 - core]
+        place = pl.ds(i * shard, shard)
+        mine_ref[:, :, place] = source[:, core]
+        theirs_ref[:, :, place] = source[:, 1 - core]
 
 
 def join_kernel(*refs):
@@ -97,57 +100,60 @@
         out_ref[:, :, i * shard : (i + 1) * shard] = part[...]
 
 
-def expert_kernel(switch_ref, own_ref, rows_ref, *refs):
-    blocks, (out_ref, weights, sem) = refs[:-3], refs[-3:]
+def stage_kernel(*refs):
+    blocks, (out_ref, sem) = refs[:-2], refs[-2:]
+    part = blocks[0].shape[2]
+    copies = [
+        pltpu.make_async_copy(block, out_ref.at[:, :, pl.ds(b * part, part)], sem.at[b])
+        for b, block in enumerate(blocks)
+    ]
+    for copy in copies:
+        copy.start()
+    for copy in copies:
+        copy.wait()
+
+
+def expert_kernel(switch_ref, own_ref, rows_ref, weights_hbm, out_ref, weights, sem):
     sources, steps, cap, width = rows_ref.shape
-    mats, part = blocks[0].shape[1:3]
+    mats = weights.shape[1]
     first_new = switch_ref[own_ref[0]]
     version_at = lambda step: (step >= first_new).astype(jnp.int32)
+    changes = (first_new > 0) & (first_new < steps)
     nt = (((1,), (1,)), ((), ()))
 
-    def copies(version, i):
-        return [
-            pltpu.make_async_copy(
-                block.at[version, i],
-                weights.at[version, i, pl.ds(b * part, part)],
-                sem.at[version, i, b],
-            )
-            for b, block in enumerate(blocks)
-        ]
-
-    def fetch(version):
+    def matrix(version, i):
+        return pltpu.make_async_copy(
+            weights_hbm.at[version, i], weights.at[version, i], sem.at[version, i]
+        )
+
+    for i in range(mats):
+        matrix(version_at(0), i).start()
+
+    @pl.when(changes)
+    def _():
         for i in range(mats):
-            for copy in copies(version, i):
-                copy.start()
-
-    def arrive(version, i):
-        for copy in copies(version, i):
-            copy.wait()
-
-    both = (first_new > 0) & (first_new < steps)
-    fetch(version_at(0))
-    pl.when(both)(lambda: fetch(1))
+            matrix(1, i).start()
+
     for step in range(steps):
         version = version_at(step)
+        rows_in = rows_ref[:, step].astype(F32).reshape(sources * cap, width).astype(BF16)
         if step == 0:
-            arrive(version, 0)
-        else:
-
-            @pl.when(first_new == step)
-            def _():
-                for i in range(mats):
-                    arrive(1, i)
-
-        rows_in = rows_ref[:, step].astype(F32).reshape(sources * cap, width).astype(BF16)
+            matrix(version, 0).wait()
         gate_v = lax.dot_general(rows_in, weights[version, 0], nt, preferred_element_type=F32)
         if step == 0:
-            arrive(version, 1)
+            matrix(version, 1).wait()
         up_v = lax.dot_general(rows_in, weights[version, 1], nt, preferred_element_type=F32)
         act = (gate_v / (1.0 + jnp.exp(-gate_v)) * up_v).astype(BF16)
         if step == 0:
-            arrive(version, 2)
+            matrix(version, 2).wait()
         made = jnp.dot(act, weights[version, 2], preferred_element_type=F32)
         out_ref[:, step] = made.reshape(sources, cap, width).astype(BF16)
+        if step == 0:
+
+            @pl.when(changes)
+            def _():
+                for i in range(mats):
+                    matrix(1, i).wait()
 
 
 def combine_kernel(hidden_ref, weights_ref, back_ref, out_ref):
@@ -196,22 +202,28 @@
             blocks, ("group", "expert"), 0, 0, axis_index_groups=rings, tiled=True
         )
 
-    partner = [move(array, 1, 0, 0) for array in (experts_old, experts_new)]
-
     far = lambda array: pltpu.with_memory_space_constraint(array, pltpu.HBM)
     routes = routes.transpose(0, 2, 1)
     gates = gates.transpose(0, 2, 1)
+    whole = pl.BlockSpec(memory_space=pltpu.VMEM)
+    inputs = (experts_old, experts_new, hidden, norm_gain.reshape(1, width), routes)
+    both, *near_inputs = pl.pallas_call(
+        load_kernel,
+        in_specs=[pl.BlockSpec(memory_space=pltpu.HBM)] * len(inputs),
+        out_specs=[whole] * (len(inputs) - 1),
+        out_shape=[pltpu.VMEM((2,) + experts_old.shape, BF16)]
+        + [pltpu.VMEM(array.shape, array.dtype) for array in inputs[2:]],
+        scratch_shapes=[pltpu.SemaphoreType.DMA((len(inputs),))],
+        compiler_params=limit(16),
+        name="load",
+    )(*(far(array) for array in inputs))
     outgoing = pl.pallas_call(
         pack_kernel,
-        in_specs=[pl.BlockSpec(memory_space=pltpu.HBM)] * 3,
+        in_specs=[whole] * 3,
         out_specs=pl.BlockSpec(memory_space=pltpu.HBM),
         out_shape=pltpu.HBM((experts, steps, CAP, width), BF16),
         scratch_shapes=[
-            pltpu.VMEM(hidden.shape, BF16),
-            pltpu.VMEM((1, width), F32),
-            pltpu.VMEM((steps, top, rows), jnp.int32),
             pltpu.VMEM((steps, experts, CAP, width), BF16),
-            pltpu.SemaphoreType.DMA((3,)),
             pltpu.SemaphoreType.DMA((steps,)),
         ],
         compiler_params=limit(16),
@@ -219,7 +231,7 @@
             flops=2 * steps * rows * slots * width, bytes_accessed=4 << 20, transcendentals=0
         ),
         name="pack",
-    )(far(hidden), far(norm_gain.reshape(1, width)), far(routes))
+    )(*near_inputs)
     weigh = pl.pallas_call(
         weigh_kernel,
         out_shape=jax.ShapeDtypeStruct((steps, 3 * rows, slots), BF16),
@@ -228,15 +240,14 @@
     )(routes, gates)
     received = exchange(outgoing)
     near = (2, mats, 2 * shard, width)
-    whole = pl.BlockSpec(memory_space=pltpu.VMEM)
     mine, theirs = pl.pallas_call(
         sort_kernel,
-        in_specs=[pl.BlockSpec(memory_space=pltpu.SMEM)] + [whole] * 4,
+        in_specs=[pl.BlockSpec(memory_space=pltpu.SMEM)] + [whole] * 2,
         out_shape=(jax.ShapeDtypeStruct(near, BF16), jax.ShapeDtypeStruct(near, BF16)),
         compiler_params=limit(16),
         cost_estimate=pl.CostEstimate(flops=100_000_000_000, bytes_accessed=4 << 20, transcendentals=0),
         name="sort",
-    )(core.reshape(1), experts_old, experts_new, *partner)
+    )(core.reshape(1), both, move(both, 1, 0, 0))
     block = pl.pallas_call(
         join_kernel,
         out_shape=jax.ShapeDtypeStruct((2, mats, 4 * shard, width), BF16),
@@ -246,23 +257,31 @@
     blocks = [block] + [move(block, 0, x, 0) for x in (2, 1, -1)]
 
     received, weigh = lax.optimization_barrier((received, weigh))
+    staged = (2, mats, shard * groups, width)
+    weights = pl.pallas_call(
+        stage_kernel,
+        in_specs=[pl.BlockSpec(memory_space=pltpu.HBM)] * len(blocks),
+        out_specs=whole,
+        out_shape=jax.ShapeDtypeStruct(staged, BF16),
+        scratch_shapes=[pltpu.SemaphoreType.DMA((len(blocks),))],
+        compiler_params=limit(16),
+        cost_estimate=pl.CostEstimate(flops=10_000_000_000, bytes_accessed=9 << 20, transcendentals=0),
+        name="stage",
+    )(*(far(part) for part in blocks))
     own = lax.axis_index("expert") * exp_dev + core
     produced = pl.pallas_call(
         expert_kernel,
         grid_spec=pltpu.PrefetchScalarGridSpec(
             num_scalar_prefetch=2,
             grid=(1,),
-            in_specs=[whole] + [pl.BlockSpec(memory_space=pltpu.HBM)] * len(blocks),
+            in_specs=[whole, pl.BlockSpec(memory_space=pltpu.HBM)],
             out_specs=whole,
-            scratch_shapes=[
-                pltpu.VMEM((2, mats, shard * groups, width), BF16),
-                pltpu.SemaphoreType.DMA((2, mats, len(blocks))),
-            ],
+            scratch_shapes=[pltpu.VMEM(staged, BF16), pltpu.SemaphoreType.DMA((2, mats))],
         ),
         out_shape=jax.ShapeDtypeStruct((experts, steps, CAP, width), BF16),
         compiler_params=limit(28),
         name="experts",
-    )(switch, own.reshape(1), received, *(far(part) for part in blocks))
+    )(switch, own.reshape(1), received, far(weights))
     returned = exchange(produced)
     return pl.pallas_call(
         combine_kernel,

time: 197 us -> 195 us (0.990)
  waiting for transfers between devices: 55.3 us -> 51.2 us
  Pallas kernels: 15.8 us -> 18.9 us
  starting transfers between devices: 36.2 us -> 33.6 us
    all_to_all x1, waiting for transfers between devices: 53.5 us -> 4.85 us  [exchange(): lax.all_to_all(blocks, ('group', 'expert'), 0, 0, axis_index_groups=rings...]
    ppermute x6 -> x5, waiting for transfers between devices: 1.85 us -> 46.3 us  [move(): return lax.ppermute(array, 'group', pairs)]
    pallas_call x1 -> x3, Pallas kernels: 3.78 us -> 7.18 us  [the longest x1 2.85 us: local(): pl.pallas_call(pack_kernel, in_specs=[whole] * 3, out_specs=pl.BlockSpec(...]
    ppermute x6 -> x5, starting transfers between devices: 20.2 us -> 18.3 us  [move(): return lax.ppermute(array, 'group', pairs)]
  transfers between devices with their start and end apart: 7 -> 6, of which waited for: 2 -> 5; matrix products, arithmetic and copies ran while one was open for 0% -> 0% of each run, Pallas kernels for 3% -> 4%
where the time goes in v5:
time: 195 us; the launch traced here: 192 us
  blocking collectives  85.9 us (44%)
  waiting for transfers between devices  51.2 us (26%)
  starting transfers between devices  33.6 us (17%)
  Pallas kernels  18.9 us (10%)
  local copies, waits for them, and re-layouts  2.15 us (1%)
    all_to_all x1, blocking collectives, exchange(): lax.all_to_all(blocks, ('group', 'expert'), 0, 0, axis_index_groups=rings...  85.9 us
    ppermute x5, waiting for transfers between devices, move(): return lax.ppermute(array, 'group', pairs)  46.3 us
    ppermute x5, starting transfers between devices, move(): return lax.ppermute(array, 'group', pairs)  18.3 us
    all_to_all x1, starting transfers between devices, exchange(): lax.all_to_all(blocks, ('group', 'expert'), 0, 0, axis_index_groups=rings...  15.3 us
    pallas_call x1, Pallas kernels, local(): pl.pallas_call(expert_kernel, grid_spec=pltpu.PrefetchScalarGridSpec(num_...  7.39 us
    all_to_all x1, waiting for transfers between devices, exchange(): lax.all_to_all(blocks, ('group', 'expert'), 0, 0, axis_index_groups=rings...  4.85 us
  transfers between devices with their start and end apart: 6, of which 5 were waited for; matrix products, arithmetic and copies ran while one was open for 0% of the time, Pallas kernels for 4%

profile of v5, /device:TPU:56, one launch (start us, length us, event | category | flops | bytes accessed | tf_op | source)
XLA Modules:
  0.0 191.9 jit_solution(2585321359434316632)
XLA Ops:
  0.0 2.0 %load.1 = (bf16[2,2,3,24,1024]{4,3,2,1,0:T(8,128)(2,1)}, bf16[3,32,1024]{2,1,0:T(8,128)(2,1)S(1)}, f32[1,1024]{1,0:T(1,128)S(1)}, s32[3,8,32]{2,1,0:T(8,128)S(1)}) custom-call(bf16[2,3,24,1024]{3,2,1,0:T(8,128)(2,1)} %old_hbm.1, bf16[2,3,24,1024]{3,2,1,0:T(8,128)(2,1)} %new_hbm.1, bf16[3,32,1024]{2,1,0:T(8,128)(2,1)} %hidden_ref.1, f32[1,1024]{1,0:T(1,128)} %bitcast.8, ...), custom_call_target="tpu_custom_call" | custom-call | tf_op jit(solution)/shard_map/load/pallas_call | solution.py:210
  2.0 4.3 %collective-permute-start = (bf16[2,2,3,24,1024]{4,3,2,1,0:T(8,128)(2,1)}, bf16[2,2,3,24,1024]{4,3,2,1,0:T(8,128)(2,1)}, u32[]{:S(2)}, u32[]{:S(2)}) collective-permute-start(bf16[2,2,3,24,1024]{4,3,2,1,0:T(8,128)(2,1)} %get-tuple-element.18.refs_0_), channel_id=1, source_target_pairs={{0,256},{32,288},{64,320},{96,352},{128,384},{160,416},{192,448},{... | collective-permute-start | bytes 1769480 | tf_op jit(solution)/shard_map/ppermute | solution.py:191
  6.3 2.8 %pack.1 = bf16[64,3,8,1024]{3,2,1,0:T(8,128)(2,1)} custom-call(bf16[3,32,1024]{2,1,0:T(8,128)(2,1)S(1)} %get-tuple-element.13.hidden, f32[1,1024]{1,0:T(1,128)S(1)} %get-tuple-element.14.gain, s32[3,8,32]{2,1,0:T(8,128)S(1)} %get-tuple-element.15.routes), custom_call_target="tpu_custom_call" | custom-call | flops 100663296 | bytes 4194304 | tf_op jit(solution)/shard_map/pack/pallas_call | solution.py:220
  9.1 15.3 %all-to-all-start = ((bf16[64,3,8,1024]{3,2,1,0:T(8,128)(2,1)}), bf16[64,3,8,1024]{3,2,1,0:T(8,128)(2,1)S(1)}, u32[]{:S(2)}, u32[]{:S(2)}) async-start(bf16[64,3,8,1024]{3,2,1,0:T(8,128)(2,1)} %pack.1), calls=%async_computation | async-start | bytes 6291456 | tf_op jit(solution)/shard_map/all_to_all | solution.py:201
  24.4 0.0 copy-start.2
  24.4 1.3 sort.1
  25.8 2.1 %collective-permute-start.1 = (bf16[2,3,48,1024]{3,2,1,0:T(8,128)(2,1)S(1)}, bf16[2,3,48,1024]{3,2,1,0:T(8,128)(2,1)S(1)}, u32[]{:S(2)}, u32[]{:S(2)}) collective-permute-start(bf16[2,3,48,1024]{3,2,1,0:T(8,128)(2,1)S(1)} %get-tuple-element.20), channel_id=1, source_target_pairs={{0,32},{32,0},{64,96},{96,64},{128,160},{160,128},{192,224},{224,1... | collective-permute-start | bytes 1769480 | tf_op jit(solution)/shard_map/ppermute | solution.py:191
  27.8 1.8 collective-permute-done.1.refs_1_
  29.7 1.1 join.1.refs_0_
  30.8 4.9 %collective-permute-start.2 = (bf16[2,3,96,1024]{3,2,1,0:T(8,128)(2,1)}, bf16[2,3,96,1024]{3,2,1,0:T(8,128)(2,1)}, u32[]{:S(2)}, u32[]{:S(2)}) collective-permute-start(bf16[2,3,96,1024]{3,2,1,0:T(8,128)(2,1)} %join.1.refs_0_), channel_id=1, source_target_pairs={{0,128},{32,160},{64,192},{96,224},{128,0},{160,32},{192,64},{224,... | collective-permute-start | bytes 3538952 | tf_op jit(solution)/shard_map/ppermute | solution.py:191
  35.7 2.5 %collective-permute-start.3 = (bf16[2,3,96,1024]{3,2,1,0:T(8,128)(2,1)}, bf16[2,3,96,1024]{3,2,1,0:T(8,128)(2,1)}, u32[]{:S(2)}, u32[]{:S(2)}) collective-permute-start(bf16[2,3,96,1024]{3,2,1,0:T(8,128)(2,1)} %join.1.refs_0_), channel_id=1, source_target_pairs={{0,64},{32,96},{64,128},{96,160},{128,192},{160,224},{192,0},{224,... | collective-permute-start | bytes 3538952 | tf_op jit(solution)/shard_map/ppermute | solution.py:191
  38.2 4.6 %collective-permute-start.4 = (bf16[2,3,96,1024]{3,2,1,0:T(8,128)(2,1)}, bf16[2,3,96,1024]{3,2,1,0:T(8,128)(2,1)}, u32[]{:S(2)}, u32[]{:S(2)}) collective-permute-start(bf16[2,3,96,1024]{3,2,1,0:T(8,128)(2,1)} %join.1.refs_0_), channel_id=1, source_target_pairs={{0,192},{32,224},{64,0},{96,32},{128,64},{160,96},{192,128},{224,1... | collective-permute-start | bytes 3538952 | tf_op jit(solution)/shard_map/ppermute | solution.py:191
  42.8 0.6 weigh.1.weights_ref
  43.4 0.0 copy-start.4
  43.4 19.9 %collective-permute-done.2.refs_1_ = bf16[2,3,96,1024]{3,2,1,0:T(8,128)(2,1)} collective-permute-done((bf16[2,3,96,1024]{3,2,1,0:T(8,128)(2,1)}, bf16[2,3,96,1024]{3,2,1,0:T(8,128)(2,1)}, u32[]{:S(2)}, u32[]{:S(2)}) %collective-permute-start.2) | collective-permute-done | bytes 1179680 | tf_op jit(solution)/shard_map/ppermute | solution.py:191
  63.3 24.4 %collective-permute-done.3.refs_2_ = bf16[2,3,96,1024]{3,2,1,0:T(8,128)(2,1)} collective-permute-done((bf16[2,3,96,1024]{3,2,1,0:T(8,128)(2,1)}, bf16[2,3,96,1024]{3,2,1,0:T(8,128)(2,1)}, u32[]{:S(2)}, u32[]{:S(2)}) %collective-permute-start.3) | collective-permute-done | bytes 1179680 | tf_op jit(solution)/shard_map/ppermute | solution.py:191
  87.8 0.1 collective-permute-done.4.refs_3_
  87.9 2.4 %stage.1.weights_hbm = bf16[2,3,384,1024]{3,2,1,0:T(8,128)(2,1)S(1)} custom-call(bf16[2,3,96,1024]{3,2,1,0:T(8,128)(2,1)} %join.1.refs_0_, bf16[2,3,96,1024]{3,2,1,0:T(8,128)(2,1)} %collective-permute-done.2.refs_1_, bf16[2,3,96,1024]{3,2,1,0:T(8,128)(2,1)} %collective-permute-done.3.refs_2_, bf16[2,3,96,1024]{3,2,1,0:T(8,128)(2,1)} %collective-permute-done.4.refs_3_), custom_call_target="tpu_custom_call" | custom-call | flops 10000000000 | bytes 9437184 | tf_op jit(solution)/shard_map/stage/pallas_call | solution.py:261
  90.3 2.1 %copy-done = bf16[2,3,384,1024]{3,2,1,0:T(8,128)(2,1)} copy-done((bf16[2,3,384,1024]{3,2,1,0:T(8,128)(2,1)}, bf16[2,3,384,1024]{3,2,1,0:T(8,128)(2,1)S(1)}, u32[]{:S(2)}) %copy-start) | copy-done | bytes 4718616
  92.4 4.9 %all-to-all-done.rows_ref = bf16[64,3,8,1024]{3,2,1,0:T(8,128)(2,1)S(1)} async-done(((bf16[64,3,8,1024]{3,2,1,0:T(8,128)(2,1)}), bf16[64,3,8,1024]{3,2,1,0:T(8,128)(2,1)S(1)}, u32[]{:S(2)}, u32[]{:S(2)}) %all-to-all-start) | async-done | bytes 3145760 | tf_op jit(solution)/shard_map/all_to_all | solution.py:201
  97.3 7.4 %experts.1 = bf16[64,3,8,1024]{3,2,1,0:T(8,128)(2,1)S(1)} custom-call(s32[64]{0:T(128)S(1)} %copy-done.4, s32[1]{0:T(128)} %bitcast.3.own_ref, bf16[64,3,8,1024]{3,2,1,0:T(8,128)(2,1)S(1)} %all-to-all-done.rows_ref, bf16[2,3,384,1024]{3,2,1,0:T(8,128)(2,1)} %copy-done), custom_call_target="tpu_custom_call" | custom-call | tf_op jit(solution)/shard_map/experts/pallas_call | solution.py:272
  104.7 0.0 copy-start.1
  104.7 85.9 %all_to_all.10.back_ref = bf16[64,3,8,1024]{3,2,1,0:T(8,128)(2,1)S(1)} all-to-all(bf16[64,3,8,1024]{3,2,1,0:T(8,128)(2,1)S(1)} %experts.1), channel_id=1, replica_groups={{0,32,257,289,258,290,3,35,4,36,261,293,262,294,7,39,8,40,265,297,266,2..., dimensions={0} | all-to-all | bytes 6291456 | tf_op jit(solution)/shard_map/all_to_all | solution.py:201
  190.6 1.3 combine.1
  (7 shorter events, 0.0 us)
Async XLA Ops:
  2.0 22.4 %collective-permute-start = (bf16[2,2,3,24,1024]{4,3,2,1,0:T(8,128)(2,1)}, bf16[2,2,3,24,1024]{4,3,2,1,0:T(8,128)(2,1)}, u32[]{:S(2)}, u32[]{:S(2)}) collective-permute-start(bf16[2,2,3,24,1024]{4,3,2,1,0:T(8,128)(2,1)} %get-tuple-element.18.refs_0_), channel_id=1, source_target_pairs={{0,256},{32,288},{64,320},{96,352},{128,384},{160,416},{192,448},{... | collective-permute-start | bytes 1769480 | tf_op jit(solution)/shard_map/ppermute | solution.py:191
  9.1 88.1 %all-to-all-start = ((bf16[64,3,8,1024]{3,2,1,0:T(8,128)(2,1)}), bf16[64,3,8,1024]{3,2,1,0:T(8,128)(2,1)S(1)}, u32[]{:S(2)}, u32[]{:S(2)}) async-start(bf16[64,3,8,1024]{3,2,1,0:T(8,128)(2,1)} %pack.1), calls=%async_computation | async-start | bytes 6291456 | tf_op jit(solution)/shard_map/all_to_all | solution.py:201
  24.4 18.4 %copy-start.2 = (s32[3,32,8]{1,2,0:T(8,128)S(1)}, s32[3,32,8]{1,2,0:T(8,128)}, u32[]{:S(2)}) copy-start(s32[3,32,8]{1,2,0:T(8,128)} %param.9) | copy-start | bytes 9220
  24.4 18.4 %copy-start.3 = (f32[3,32,8]{1,2,0:T(8,128)S(1)}, f32[3,32,8]{1,2,0:T(8,128)}, u32[]{:S(2)}) copy-start(f32[3,32,8]{1,2,0:T(8,128)} %param.10) | copy-start | bytes 9220
  25.8 3.9 %collective-permute-start.1 = (bf16[2,3,48,1024]{3,2,1,0:T(8,128)(2,1)S(1)}, bf16[2,3,48,1024]{3,2,1,0:T(8,128)(2,1)S(1)}, u32[]{:S(2)}, u32[]{:S(2)}) collective-permute-start(bf16[2,3,48,1024]{3,2,1,0:T(8,128)(2,1)S(1)} %get-tuple-element.20), channel_id=1, source_target_pairs={{0,32},{32,0},{64,96},{96,64},{128,160},{160,128},{192,224},{224,1... | collective-permute-start | bytes 1769480 | tf_op jit(solution)/shard_map/ppermute | solution.py:191
  30.8 32.6 %collective-permute-start.2 = (bf16[2,3,96,1024]{3,2,1,0:T(8,128)(2,1)}, bf16[2,3,96,1024]{3,2,1,0:T(8,128)(2,1)}, u32[]{:S(2)}, u32[]{:S(2)}) collective-permute-start(bf16[2,3,96,1024]{3,2,1,0:T(8,128)(2,1)} %join.1.refs_0_), channel_id=1, source_target_pairs={{0,128},{32,160},{64,192},{96,224},{128,0},{160,32},{192,64},{224,... | collective-permute-start | bytes 3538952 | tf_op jit(solution)/shard_map/ppermute | solution.py:191
  35.7 52.1 %collective-permute-start.3 = (bf16[2,3,96,1024]{3,2,1,0:T(8,128)(2,1)}, bf16[2,3,96,1024]{3,2,1,0:T(8,128)(2,1)}, u32[]{:S(2)}, u32[]{:S(2)}) collective-permute-start(bf16[2,3,96,1024]{3,2,1,0:T(8,128)(2,1)} %join.1.refs_0_), channel_id=1, source_target_pairs={{0,64},{32,96},{64,128},{96,160},{128,192},{160,224},{192,0},{224,... | collective-permute-start | bytes 3538952 | tf_op jit(solution)/shard_map/ppermute | solution.py:191
  38.2 49.7 %collective-permute-start.4 = (bf16[2,3,96,1024]{3,2,1,0:T(8,128)(2,1)}, bf16[2,3,96,1024]{3,2,1,0:T(8,128)(2,1)}, u32[]{:S(2)}, u32[]{:S(2)}) collective-permute-start(bf16[2,3,96,1024]{3,2,1,0:T(8,128)(2,1)} %join.1.refs_0_), channel_id=1, source_target_pairs={{0,192},{32,224},{64,0},{96,32},{128,64},{160,96},{192,128},{224,1... | collective-permute-start | bytes 3538952 | tf_op jit(solution)/shard_map/ppermute | solution.py:191
  43.4 53.9 %copy-start.4 = (s32[64]{0:T(128)S(1)}, s32[64]{0:T(128)}, u32[]{:S(2)}) copy-start(s32[64]{0:T(128)} %switch_ref.1) | copy-start | bytes 772
  90.3 2.1 %copy-start = (bf16[2,3,384,1024]{3,2,1,0:T(8,128)(2,1)}, bf16[2,3,384,1024]{3,2,1,0:T(8,128)(2,1)S(1)}, u32[]{:S(2)}) copy-start(bf16[2,3,384,1024]{3,2,1,0:T(8,128)(2,1)S(1)} %stage.1.weights_hbm) | copy-start | bytes 14155780
  104.7 85.9 %copy-start.1 = (bf16[3,32,1024]{2,1,0:T(8,128)(2,1)S(1)}, bf16[3,32,1024]{2,1,0:T(8,128)(2,1)}, u32[]{:S(2)}) copy-start(bf16[3,32,1024]{2,1,0:T(8,128)(2,1)} %hidden_ref.1) | copy-start | bytes 589828

commit v6 on v5

--- a/solution.py
+++ b/solution.py
@@ -190,7 +190,7 @@
         ]
         return lax.ppermute(array, "group", pairs)
 
-    bend = lambda e: (e + 1) % 4 // 2
+    bend = lambda e: e % 4 // 2
     rings = [
         [device(low + bend(e), x, c) * members + e for e in range(members) for c in range(2)]
         for low in range(2)

time: 195 us -> 192 us (0.985)
  no operation moved by 1% of the time
where the time goes in v6:
time: 192 us; the launch traced here: 189 us
  blocking collectives  84.3 us (44%)
  waiting for transfers between devices  50.9 us (27%)
  starting transfers between devices  32.7 us (17%)
  Pallas kernels  18.9 us (10%)
  local copies, waits for them, and re-layouts  2.15 us (1%)
    all_to_all x1, blocking collectives, exchange(): lax.all_to_all(blocks, ('group', 'expert'), 0, 0, axis_index_groups=rings...  84.3 us
    ppermute x5, waiting for transfers between devices, move(): return lax.ppermute(array, 'group', pairs)  46.3 us
    ppermute x5, starting transfers between devices, move(): return lax.ppermute(array, 'group', pairs)  18.3 us
    all_to_all x1, starting transfers between devices, exchange(): lax.all_to_all(blocks, ('group', 'expert'), 0, 0, axis_index_groups=rings...  14.4 us
    pallas_call x1, Pallas kernels, local(): pl.pallas_call(expert_kernel, grid_spec=pltpu.PrefetchScalarGridSpec(num_...  7.4 us
    all_to_all x1, waiting for transfers between devices, exchange(): lax.all_to_all(blocks, ('group', 'expert'), 0, 0, axis_index_groups=rings...  4.53 us
  transfers between devices with their start and end apart: 6, of which 5 were waited for; matrix products, arithmetic and copies ran while one was open for 0% of the time, Pallas kernels for 4%

profile of v6, /device:TPU:56, one launch (start us, length us, event | category | flops | bytes accessed | tf_op | source)
XLA Modules:
  0.0 189.0 jit_solution(16171912555421716758)
XLA Ops:
  0.0 2.0 %load.1 = (bf16[2,2,3,24,1024]{4,3,2,1,0:T(8,128)(2,1)}, bf16[3,32,1024]{2,1,0:T(8,128)(2,1)S(1)}, f32[1,1024]{1,0:T(1,128)S(1)}, s32[3,8,32]{2,1,0:T(8,128)S(1)}) custom-call(bf16[2,3,24,1024]{3,2,1,0:T(8,128)(2,1)} %old_hbm.1, bf16[2,3,24,1024]{3,2,1,0:T(8,128)(2,1)} %new_hbm.1, bf16[3,32,1024]{2,1,0:T(8,128)(2,1)} %hidden_ref.1, f32[1,1024]{1,0:T(1,128)} %bitcast.8, ...), custom_call_target="tpu_custom_call" | custom-call | tf_op jit(solution)/shard_map/load/pallas_call | solution.py:210
  2.0 4.3 %collective-permute-start = (bf16[2,2,3,24,1024]{4,3,2,1,0:T(8,128)(2,1)}, bf16[2,2,3,24,1024]{4,3,2,1,0:T(8,128)(2,1)}, u32[]{:S(2)}, u32[]{:S(2)}) collective-permute-start(bf16[2,2,3,24,1024]{4,3,2,1,0:T(8,128)(2,1)} %get-tuple-element.18.refs_0_), channel_id=1, source_target_pairs={{0,256},{32,288},{64,320},{96,352},{128,384},{160,416},{192,448},{... | collective-permute-start | bytes 1769480 | tf_op jit(solution)/shard_map/ppermute | solution.py:191
  6.3 2.8 %pack.1 = bf16[64,3,8,1024]{3,2,1,0:T(8,128)(2,1)} custom-call(bf16[3,32,1024]{2,1,0:T(8,128)(2,1)S(1)} %get-tuple-element.13.hidden, f32[1,1024]{1,0:T(1,128)S(1)} %get-tuple-element.14.gain, s32[3,8,32]{2,1,0:T(8,128)S(1)} %get-tuple-element.15.routes), custom_call_target="tpu_custom_call" | custom-call | flops 100663296 | bytes 4194304 | tf_op jit(solution)/shard_map/pack/pallas_call | solution.py:220
  9.1 14.4 %all-to-all-start = ((bf16[64,3,8,1024]{3,2,1,0:T(8,128)(2,1)}), bf16[64,3,8,1024]{3,2,1,0:T(8,128)(2,1)S(1)}, u32[]{:S(2)}, u32[]{:S(2)}) async-start(bf16[64,3,8,1024]{3,2,1,0:T(8,128)(2,1)} %pack.1), calls=%async_computation | async-start | bytes 6291456 | tf_op jit(solution)/shard_map/all_to_all | solution.py:201
  23.5 0.0 copy-start.2
  23.5 0.0 copy-start.3
  23.5 1.3 sort.1
  24.9 2.1 %collective-permute-start.1 = (bf16[2,3,48,1024]{3,2,1,0:T(8,128)(2,1)S(1)}, bf16[2,3,48,1024]{3,2,1,0:T(8,128)(2,1)S(1)}, u32[]{:S(2)}, u32[]{:S(2)}) collective-permute-start(bf16[2,3,48,1024]{3,2,1,0:T(8,128)(2,1)S(1)} %get-tuple-element.20), channel_id=1, source_target_pairs={{0,32},{32,0},{64,96},{96,64},{128,160},{160,128},{192,224},{224,1... | collective-permute-start | bytes 1769480 | tf_op jit(solution)/shard_map/ppermute | solution.py:191
  26.9 1.8 collective-permute-done.1.refs_1_
  28.8 1.1 join.1.refs_0_
  29.9 4.9 %collective-permute-start.2 = (bf16[2,3,96,1024]{3,2,1,0:T(8,128)(2,1)}, bf16[2,3,96,1024]{3,2,1,0:T(8,128)(2,1)}, u32[]{:S(2)}, u32[]{:S(2)}) collective-permute-start(bf16[2,3,96,1024]{3,2,1,0:T(8,128)(2,1)} %join.1.refs_0_), channel_id=1, source_target_pairs={{0,128},{32,160},{64,192},{96,224},{128,0},{160,32},{192,64},{224,... | collective-permute-start | bytes 3538952 | tf_op jit(solution)/shard_map/ppermute | solution.py:191
  34.8 2.5 %collective-permute-start.3 = (bf16[2,3,96,1024]{3,2,1,0:T(8,128)(2,1)}, bf16[2,3,96,1024]{3,2,1,0:T(8,128)(2,1)}, u32[]{:S(2)}, u32[]{:S(2)}) collective-permute-start(bf16[2,3,96,1024]{3,2,1,0:T(8,128)(2,1)} %join.1.refs_0_), channel_id=1, source_target_pairs={{0,64},{32,96},{64,128},{96,160},{128,192},{160,224},{192,0},{224,... | collective-permute-start | bytes 3538952 | tf_op jit(solution)/shard_map/ppermute | solution.py:191
  37.3 4.6 %collective-permute-start.4 = (bf16[2,3,96,1024]{3,2,1,0:T(8,128)(2,1)}, bf16[2,3,96,1024]{3,2,1,0:T(8,128)(2,1)}, u32[]{:S(2)}, u32[]{:S(2)}) collective-permute-start(bf16[2,3,96,1024]{3,2,1,0:T(8,128)(2,1)} %join.1.refs_0_), channel_id=1, source_target_pairs={{0,192},{32,224},{64,0},{96,32},{128,64},{160,96},{192,128},{224,1... | collective-permute-start | bytes 3538952 | tf_op jit(solution)/shard_map/ppermute | solution.py:191
  41.9 0.6 weigh.1.weights_ref
  42.5 19.9 %collective-permute-done.2.refs_1_ = bf16[2,3,96,1024]{3,2,1,0:T(8,128)(2,1)} collective-permute-done((bf16[2,3,96,1024]{3,2,1,0:T(8,128)(2,1)}, bf16[2,3,96,1024]{3,2,1,0:T(8,128)(2,1)}, u32[]{:S(2)}, u32[]{:S(2)}) %collective-permute-start.2) | collective-permute-done | bytes 1179680 | tf_op jit(solution)/shard_map/ppermute | solution.py:191
  62.4 24.4 %collective-permute-done.3.refs_2_ = bf16[2,3,96,1024]{3,2,1,0:T(8,128)(2,1)} collective-permute-done((bf16[2,3,96,1024]{3,2,1,0:T(8,128)(2,1)}, bf16[2,3,96,1024]{3,2,1,0:T(8,128)(2,1)}, u32[]{:S(2)}, u32[]{:S(2)}) %collective-permute-start.3) | collective-permute-done | bytes 1179680 | tf_op jit(solution)/shard_map/ppermute | solution.py:191
  86.9 0.1 collective-permute-done.4.refs_3_
  87.0 2.4 %stage.1.weights_hbm = bf16[2,3,384,1024]{3,2,1,0:T(8,128)(2,1)S(1)} custom-call(bf16[2,3,96,1024]{3,2,1,0:T(8,128)(2,1)} %join.1.refs_0_, bf16[2,3,96,1024]{3,2,1,0:T(8,128)(2,1)} %collective-permute-done.2.refs_1_, bf16[2,3,96,1024]{3,2,1,0:T(8,128)(2,1)} %collective-permute-done.3.refs_2_, bf16[2,3,96,1024]{3,2,1,0:T(8,128)(2,1)} %collective-permute-done.4.refs_3_), custom_call_target="tpu_custom_call" | custom-call | flops 10000000000 | bytes 9437184 | tf_op jit(solution)/shard_map/stage/pallas_call | solution.py:261
  89.4 2.1 %copy-done = bf16[2,3,384,1024]{3,2,1,0:T(8,128)(2,1)} copy-done((bf16[2,3,384,1024]{3,2,1,0:T(8,128)(2,1)}, bf16[2,3,384,1024]{3,2,1,0:T(8,128)(2,1)S(1)}, u32[]{:S(2)}) %copy-start) | copy-done | bytes 4718616
  91.5 4.5 %all-to-all-done.rows_ref = bf16[64,3,8,1024]{3,2,1,0:T(8,128)(2,1)S(1)} async-done(((bf16[64,3,8,1024]{3,2,1,0:T(8,128)(2,1)}), bf16[64,3,8,1024]{3,2,1,0:T(8,128)(2,1)S(1)}, u32[]{:S(2)}, u32[]{:S(2)}) %all-to-all-start) | async-done | bytes 3145760 | tf_op jit(solution)/shard_map/all_to_all | solution.py:201
  96.0 7.4 %experts.1 = bf16[64,3,8,1024]{3,2,1,0:T(8,128)(2,1)S(1)} custom-call(s32[64]{0:T(128)S(1)} %copy-done.4, s32[1]{0:T(128)} %bitcast.3.own_ref, bf16[64,3,8,1024]{3,2,1,0:T(8,128)(2,1)S(1)} %all-to-all-done.rows_ref, bf16[2,3,384,1024]{3,2,1,0:T(8,128)(2,1)} %copy-done), custom_call_target="tpu_custom_call" | custom-call | tf_op jit(solution)/shard_map/experts/pallas_call | solution.py:272
  103.4 0.0 copy-start.1
  103.4 84.3 %all_to_all.10.back_ref = bf16[64,3,8,1024]{3,2,1,0:T(8,128)(2,1)S(1)} all-to-all(bf16[64,3,8,1024]{3,2,1,0:T(8,128)(2,1)S(1)} %experts.1), channel_id=1, replica_groups={{0,32,1,33,258,290,259,291,4,36,5,37,262,294,263,295,8,40,9,41,266,298,..., dimensions={0} | all-to-all | bytes 6291456 | tf_op jit(solution)/shard_map/all_to_all | solution.py:201
  187.7 1.3 combine.1
  (7 shorter events, 0.0 us)
Async XLA Ops:
  2.0 21.5 %collective-permute-start = (bf16[2,2,3,24,1024]{4,3,2,1,0:T(8,128)(2,1)}, bf16[2,2,3,24,1024]{4,3,2,1,0:T(8,128)(2,1)}, u32[]{:S(2)}, u32[]{:S(2)}) collective-permute-start(bf16[2,2,3,24,1024]{4,3,2,1,0:T(8,128)(2,1)} %get-tuple-element.18.refs_0_), channel_id=1, source_target_pairs={{0,256},{32,288},{64,320},{96,352},{128,384},{160,416},{192,448},{... | collective-permute-start | bytes 1769480 | tf_op jit(solution)/shard_map/ppermute | solution.py:191
  9.1 86.9 %all-to-all-start = ((bf16[64,3,8,1024]{3,2,1,0:T(8,128)(2,1)}), bf16[64,3,8,1024]{3,2,1,0:T(8,128)(2,1)S(1)}, u32[]{:S(2)}, u32[]{:S(2)}) async-start(bf16[64,3,8,1024]{3,2,1,0:T(8,128)(2,1)} %pack.1), calls=%async_computation | async-start | bytes 6291456 | tf_op jit(solution)/shard_map/all_to_all | solution.py:201
  23.5 18.4 %copy-start.2 = (s32[3,32,8]{1,2,0:T(8,128)S(1)}, s32[3,32,8]{1,2,0:T(8,128)}, u32[]{:S(2)}) copy-start(s32[3,32,8]{1,2,0:T(8,128)} %param.9) | copy-start | bytes 9220
  23.5 18.4 %copy-start.3 = (f32[3,32,8]{1,2,0:T(8,128)S(1)}, f32[3,32,8]{1,2,0:T(8,128)}, u32[]{:S(2)}) copy-start(f32[3,32,8]{1,2,0:T(8,128)} %param.10) | copy-start | bytes 9220
  24.9 3.9 %collective-permute-start.1 = (bf16[2,3,48,1024]{3,2,1,0:T(8,128)(2,1)S(1)}, bf16[2,3,48,1024]{3,2,1,0:T(8,128)(2,1)S(1)}, u32[]{:S(2)}, u32[]{:S(2)}) collective-permute-start(bf16[2,3,48,1024]{3,2,1,0:T(8,128)(2,1)S(1)} %get-tuple-element.20), channel_id=1, source_target_pairs={{0,32},{32,0},{64,96},{96,64},{128,160},{160,128},{192,224},{224,1... | collective-permute-start | bytes 1769480 | tf_op jit(solution)/shard_map/ppermute | solution.py:191
  29.9 32.6 %collective-permute-start.2 = (bf16[2,3,96,1024]{3,2,1,0:T(8,128)(2,1)}, bf16[2,3,96,1024]{3,2,1,0:T(8,128)(2,1)}, u32[]{:S(2)}, u32[]{:S(2)}) collective-permute-start(bf16[2,3,96,1024]{3,2,1,0:T(8,128)(2,1)} %join.1.refs_0_), channel_id=1, source_target_pairs={{0,128},{32,160},{64,192},{96,224},{128,0},{160,32},{192,64},{224,... | collective-permute-start | bytes 3538952 | tf_op jit(solution)/shard_map/ppermute | solution.py:191
  34.8 52.1 %collective-permute-start.3 = (bf16[2,3,96,1024]{3,2,1,0:T(8,128)(2,1)}, bf16[2,3,96,1024]{3,2,1,0:T(8,128)(2,1)}, u32[]{:S(2)}, u32[]{:S(2)}) collective-permute-start(bf16[2,3,96,1024]{3,2,1,0:T(8,128)(2,1)} %join.1.refs_0_), channel_id=1, source_target_pairs={{0,64},{32,96},{64,128},{96,160},{128,192},{160,224},{192,0},{224,... | collective-permute-start | bytes 3538952 | tf_op jit(solution)/shard_map/ppermute | solution.py:191
  37.3 49.7 %collective-permute-start.4 = (bf16[2,3,96,1024]{3,2,1,0:T(8,128)(2,1)}, bf16[2,3,96,1024]{3,2,1,0:T(8,128)(2,1)}, u32[]{:S(2)}, u32[]{:S(2)}) collective-permute-start(bf16[2,3,96,1024]{3,2,1,0:T(8,128)(2,1)} %join.1.refs_0_), channel_id=1, source_target_pairs={{0,192},{32,224},{64,0},{96,32},{128,64},{160,96},{192,128},{224,1... | collective-permute-start | bytes 3538952 | tf_op jit(solution)/shard_map/ppermute | solution.py:191
  42.5 53.5 %copy-start.4 = (s32[64]{0:T(128)S(1)}, s32[64]{0:T(128)}, u32[]{:S(2)}) copy-start(s32[64]{0:T(128)} %switch_ref.1) | copy-start | bytes 772
  89.4 2.1 %copy-start = (bf16[2,3,384,1024]{3,2,1,0:T(8,128)(2,1)}, bf16[2,3,384,1024]{3,2,1,0:T(8,128)(2,1)S(1)}, u32[]{:S(2)}) copy-start(bf16[2,3,384,1024]{3,2,1,0:T(8,128)(2,1)S(1)} %stage.1.weights_hbm) | copy-start | bytes 14155780
  103.4 84.3 %copy-start.1 = (bf16[3,32,1024]{2,1,0:T(8,128)(2,1)S(1)}, bf16[3,32,1024]{2,1,0:T(8,128)(2,1)}, u32[]{:S(2)}) copy-start(bf16[3,32,1024]{2,1,0:T(8,128)(2,1)} %hidden_ref.1) | copy-start | bytes 589828

commit v7 on v6

--- a/solution.py
+++ b/solution.py
@@ -27,7 +27,9 @@
     return named & (rank == (lane & 7).astype(F32))
 
 
-def load_kernel(old_hbm, new_hbm, hidden_hbm, gain_hbm, routes_hbm, both, hidden, gain, routes, sem):
+def load_kernel(
+    old_hbm, new_hbm, hidden_hbm, gain_hbm, routes_hbm, both_hbm, hidden, gain, routes, both, sem, out_sem
+):
     moves = (
         (old_hbm, both.at[0]),
         (new_hbm, both.at[1]),
@@ -40,7 +42,15 @@
     ]
     for copy in copies:
         copy.start()
-    for copy in copies:
+    leaving = [
+        pltpu.make_async_copy(both.at[i], both_hbm.at[i], out_sem.at[i]) for i in range(2)
+    ]
+    for i in range(2):
+        copies[i].wait()
+        leaving[i].start()
+    for copy in copies[2:]:
+        copy.wait()
+    for copy in leaving:
         copy.wait()
 
 
@@ -52,12 +62,22 @@
         scale = lax.rsqrt(jnp.mean(xf * xf, axis=-1, keepdims=True) + 1e-06)
         normed = (xf * scale * gain[...]).astype(BF16)
         spread = slot_mask(routes[step].T, experts).astype(F32).astype(BF16)
-        rows_out = lax.dot_general(
-            spread, normed, (((0,), (0,)), ((), ())), preferred_element_type=F32
-        )
-        packed[step] = rows_out.reshape(experts, cap, width).astype(BF16)
-        leaving.append(pltpu.make_async_copy(packed.at[step], out_hbm.at[:, step], sem.at[step]))
-        leaving[-1].start()
+        half = experts // 2
+        for i in range(2):
+            rows_out = lax.dot_general(
+                spread[:, i * half * cap : (i + 1) * half * cap],
+                normed,
+                (((0,), (0,)), ((), ())),
+                preferred_element_type=F32,
+            )
+            place = pl.ds(i * half, half)
+            packed[step, place] = rows_out.reshape(half, cap, width).astype(BF16)
+            leaving.append(
+                pltpu.make_async_copy(
+                    packed.at[step, place], out_hbm.at[place, step], sem.at[step, i]
+                )
+            )
+            leaving[-1].start()
     for copy in leaving:
         copy.wait()
 
@@ -146,15 +166,14 @@
         act = (gate_v / (1.0 + jnp.exp(-gate_v)) * up_v).astype(BF16)
         if step == 0:
             matrix(version, 2).wait()
-        made = jnp.dot(act, weights[version, 2], preferred_element_type=F32)
-        out_ref[:, step] = made.reshape(sources, cap, width).astype(BF16)
-        if step == 0:
 
             @pl.when(changes)
             def _():
                 for i in range(mats):
                     matrix(1, i).wait()
 
+        made = jnp.dot(act, weights[version, 2], preferred_element_type=F32)
+        out_ref[:, step] = made.reshape(sources, cap, width).astype(BF16)
 
 def combine_kernel(hidden_ref, weights_ref, back_ref, out_ref):
     steps, rows, width = hidden_ref.shape
@@ -210,10 +229,14 @@
     both, *near_inputs = pl.pallas_call(
         load_kernel,
         in_specs=[pl.BlockSpec(memory_space=pltpu.HBM)] * len(inputs),
-        out_specs=[whole] * (len(inputs) - 1),
-        out_shape=[pltpu.VMEM((2,) + experts_old.shape, BF16)]
+        out_specs=[pl.BlockSpec(memory_space=pltpu.HBM)] + [whole] * (len(inputs) - 2),
+        out_shape=[pltpu.HBM((2,) + experts_old.shape, BF16)]
         + [pltpu.VMEM(array.shape, array.dtype) for array in inputs[2:]],
-        scratch_shapes=[pltpu.SemaphoreType.DMA((len(inputs),))],
+        scratch_shapes=[
+            pltpu.VMEM((2,) + experts_old.shape, BF16),
+            pltpu.SemaphoreType.DMA((len(inputs),)),
+            pltpu.SemaphoreType.DMA((2,)),
+        ],
         compiler_params=limit(16),
         name="load",
     )(*(far(array) for array in inputs))
@@ -224,7 +247,7 @@
         out_shape=pltpu.HBM((experts, steps, CAP, width), BF16),
         scratch_shapes=[
             pltpu.VMEM((steps, experts, CAP, width), BF16),
-            pltpu.SemaphoreType.DMA((steps,)),
+            pltpu.SemaphoreType.DMA((steps, 2)),
         ],
         compiler_params=limit(16),
         cost_estimate=pl.CostEstimate(

time: 192 us -> 192 us (level)
  no operation moved by 1% of the time
where the time goes in v7:
time: 192 us; the launch traced here: 189 us
  blocking collectives  84.3 us (44%)
  waiting for transfers between devices  50 us (26%)
  starting transfers between devices  32.7 us (17%)
  Pallas kernels  18.3 us (10%)
  local copies, waits for them, and re-layouts  3.19 us (2%)
    all_to_all x1, blocking collectives, exchange(): lax.all_to_all(blocks, ('group', 'expert'), 0, 0, axis_index_groups=rings...  84.3 us
    ppermute x5, waiting for transfers between devices, move(): return lax.ppermute(array, 'group', pairs)  46.3 us
    ppermute x5, starting transfers between devices, move(): return lax.ppermute(array, 'group', pairs)  18.3 us
    all_to_all x1, starting transfers between devices, exchange(): lax.all_to_all(blocks, ('group', 'expert'), 0, 0, axis_index_groups=rings...  14.4 us
    pallas_call x1, Pallas kernels, local(): pl.pallas_call(expert_kernel, grid_spec=pltpu.PrefetchScalarGridSpec(num_...  7.2 us
  transfers between devices with their start and end apart: 6, of which 5 were waited for; matrix products, arithmetic and copies ran while one was open for 0% of the time, Pallas kernels for 4%

profile of v7, /device:TPU:56, one launch (start us, length us, event | category | flops | bytes accessed | tf_op | source)
XLA Modules:
  0.0 188.6 jit_solution(9790832431549043169)
XLA Ops:
  0.0 1.8 load.1
  1.9 4.3 %collective-permute-start = (bf16[2,2,3,24,1024]{4,3,2,1,0:T(8,128)(2,1)}, bf16[2,2,3,24,1024]{4,3,2,1,0:T(8,128)(2,1)}, u32[]{:S(2)}, u32[]{:S(2)}) collective-permute-start(bf16[2,2,3,24,1024]{4,3,2,1,0:T(8,128)(2,1)} %get-tuple-element.18.refs_0_), channel_id=1, source_target_pairs={{0,256},{32,288},{64,320},{96,352},{128,384},{160,416},{192,448},{... | collective-permute-start | bytes 1769480 | tf_op jit(solution)/shard_map/ppermute | solution.py:210
  6.1 2.7 %pack.1 = bf16[64,3,8,1024]{3,2,1,0:T(8,128)(2,1)} custom-call(bf16[3,32,1024]{2,1,0:T(8,128)(2,1)S(1)} %get-tuple-element.13.hidden, f32[1,1024]{1,0:T(1,128)S(1)} %get-tuple-element.14.gain, s32[3,8,32]{2,1,0:T(8,128)S(1)} %get-tuple-element.15.routes), custom_call_target="tpu_custom_call" | custom-call | flops 100663296 | bytes 4194304 | tf_op jit(solution)/shard_map/pack/pallas_call | solution.py:243
  8.9 14.4 %all-to-all-start = ((bf16[64,3,8,1024]{3,2,1,0:T(8,128)(2,1)}), bf16[64,3,8,1024]{3,2,1,0:T(8,128)(2,1)S(1)}, u32[]{:S(2)}, u32[]{:S(2)}) async-start(bf16[64,3,8,1024]{3,2,1,0:T(8,128)(2,1)} %pack.1), calls=%async_computation | async-start | bytes 6291456 | tf_op jit(solution)/shard_map/all_to_all | solution.py:220
  23.3 1.1 copy-done.5
  24.3 1.2 sort.1
  25.5 2.1 %collective-permute-start.1 = (bf16[2,3,48,1024]{3,2,1,0:T(8,128)(2,1)S(1)}, bf16[2,3,48,1024]{3,2,1,0:T(8,128)(2,1)S(1)}, u32[]{:S(2)}, u32[]{:S(2)}) collective-permute-start(bf16[2,3,48,1024]{3,2,1,0:T(8,128)(2,1)S(1)} %get-tuple-element.20), channel_id=1, source_target_pairs={{0,32},{32,0},{64,96},{96,64},{128,160},{160,128},{192,224},{224,1... | collective-permute-start | bytes 1769480 | tf_op jit(solution)/shard_map/ppermute | solution.py:210
  27.6 1.8 collective-permute-done.1.refs_1_
  29.4 1.1 join.1.refs_0_
  30.5 4.9 %collective-permute-start.2 = (bf16[2,3,96,1024]{3,2,1,0:T(8,128)(2,1)}, bf16[2,3,96,1024]{3,2,1,0:T(8,128)(2,1)}, u32[]{:S(2)}, u32[]{:S(2)}) collective-permute-start(bf16[2,3,96,1024]{3,2,1,0:T(8,128)(2,1)} %join.1.refs_0_), channel_id=1, source_target_pairs={{0,128},{32,160},{64,192},{96,224},{128,0},{160,32},{192,64},{224,... | collective-permute-start | bytes 3538952 | tf_op jit(solution)/shard_map/ppermute | solution.py:210
  35.4 2.5 %collective-permute-start.3 = (bf16[2,3,96,1024]{3,2,1,0:T(8,128)(2,1)}, bf16[2,3,96,1024]{3,2,1,0:T(8,128)(2,1)}, u32[]{:S(2)}, u32[]{:S(2)}) collective-permute-start(bf16[2,3,96,1024]{3,2,1,0:T(8,128)(2,1)} %join.1.refs_0_), channel_id=1, source_target_pairs={{0,64},{32,96},{64,128},{96,160},{128,192},{160,224},{192,0},{224,... | collective-permute-start | bytes 3538952 | tf_op jit(solution)/shard_map/ppermute | solution.py:210
  38.0 4.5 %collective-permute-start.4 = (bf16[2,3,96,1024]{3,2,1,0:T(8,128)(2,1)}, bf16[2,3,96,1024]{3,2,1,0:T(8,128)(2,1)}, u32[]{:S(2)}, u32[]{:S(2)}) collective-permute-start(bf16[2,3,96,1024]{3,2,1,0:T(8,128)(2,1)} %join.1.refs_0_), channel_id=1, source_target_pairs={{0,192},{32,224},{64,0},{96,32},{128,64},{160,96},{192,128},{224,1... | collective-permute-start | bytes 3538952 | tf_op jit(solution)/shard_map/ppermute | solution.py:210
  42.5 0.6 weigh.1.weights_ref
  43.1 0.0 copy-start.4
  43.2 19.9 %collective-permute-done.2.refs_1_ = bf16[2,3,96,1024]{3,2,1,0:T(8,128)(2,1)} collective-permute-done((bf16[2,3,96,1024]{3,2,1,0:T(8,128)(2,1)}, bf16[2,3,96,1024]{3,2,1,0:T(8,128)(2,1)}, u32[]{:S(2)}, u32[]{:S(2)}) %collective-permute-start.2) | collective-permute-done | bytes 1179680 | tf_op jit(solution)/shard_map/ppermute | solution.py:210
  63.1 24.4 %collective-permute-done.3.refs_2_ = bf16[2,3,96,1024]{3,2,1,0:T(8,128)(2,1)} collective-permute-done((bf16[2,3,96,1024]{3,2,1,0:T(8,128)(2,1)}, bf16[2,3,96,1024]{3,2,1,0:T(8,128)(2,1)}, u32[]{:S(2)}, u32[]{:S(2)}) %collective-permute-start.3) | collective-permute-done | bytes 1179680 | tf_op jit(solution)/shard_map/ppermute | solution.py:210
  87.5 0.1 collective-permute-done.4.refs_3_
  87.7 2.4 %stage.1.weights_hbm = bf16[2,3,384,1024]{3,2,1,0:T(8,128)(2,1)S(1)} custom-call(bf16[2,3,96,1024]{3,2,1,0:T(8,128)(2,1)} %join.1.refs_0_, bf16[2,3,96,1024]{3,2,1,0:T(8,128)(2,1)} %collective-permute-done.2.refs_1_, bf16[2,3,96,1024]{3,2,1,0:T(8,128)(2,1)} %collective-permute-done.3.refs_2_, bf16[2,3,96,1024]{3,2,1,0:T(8,128)(2,1)} %collective-permute-done.4.refs_3_), custom_call_target="tpu_custom_call" | custom-call | flops 10000000000 | bytes 9437184 | tf_op jit(solution)/shard_map/stage/pallas_call | solution.py:284
  90.0 2.1 %copy-done = bf16[2,3,384,1024]{3,2,1,0:T(8,128)(2,1)} copy-done((bf16[2,3,384,1024]{3,2,1,0:T(8,128)(2,1)}, bf16[2,3,384,1024]{3,2,1,0:T(8,128)(2,1)S(1)}, u32[]{:S(2)}) %copy-start) | copy-done | bytes 4718616
  92.2 3.6 %all-to-all-done.rows_ref = bf16[64,3,8,1024]{3,2,1,0:T(8,128)(2,1)S(1)} async-done(((bf16[64,3,8,1024]{3,2,1,0:T(8,128)(2,1)}), bf16[64,3,8,1024]{3,2,1,0:T(8,128)(2,1)S(1)}, u32[]{:S(2)}, u32[]{:S(2)}) %all-to-all-start) | async-done | bytes 3145760 | tf_op jit(solution)/shard_map/all_to_all | solution.py:220
  95.8 7.2 %experts.1 = bf16[64,3,8,1024]{3,2,1,0:T(8,128)(2,1)S(1)} custom-call(s32[64]{0:T(128)S(1)} %copy-done.4, s32[1]{0:T(128)} %bitcast.3.own_ref, bf16[64,3,8,1024]{3,2,1,0:T(8,128)(2,1)S(1)} %all-to-all-done.rows_ref, bf16[2,3,384,1024]{3,2,1,0:T(8,128)(2,1)} %copy-done), custom_call_target="tpu_custom_call" | custom-call | tf_op jit(solution)/shard_map/experts/pallas_call | solution.py:295
  103.0 0.0 copy-start.1
  103.0 84.3 %all_to_all.10.back_ref = bf16[64,3,8,1024]{3,2,1,0:T(8,128)(2,1)S(1)} all-to-all(bf16[64,3,8,1024]{3,2,1,0:T(8,128)(2,1)S(1)} %experts.1), channel_id=1, replica_groups={{0,32,1,33,258,290,259,291,4,36,5,37,262,294,263,295,8,40,9,41,266,298,..., dimensions={0} | all-to-all | bytes 6291456 | tf_op jit(solution)/shard_map/all_to_all | solution.py:220
  187.3 1.3 combine.1
  (9 shorter events, 0.0 us)
Async XLA Ops:
  1.9 21.4 %collective-permute-start = (bf16[2,2,3,24,1024]{4,3,2,1,0:T(8,128)(2,1)}, bf16[2,2,3,24,1024]{4,3,2,1,0:T(8,128)(2,1)}, u32[]{:S(2)}, u32[]{:S(2)}) collective-permute-start(bf16[2,2,3,24,1024]{4,3,2,1,0:T(8,128)(2,1)} %get-tuple-element.18.refs_0_), channel_id=1, source_target_pairs={{0,256},{32,288},{64,320},{96,352},{128,384},{160,416},{192,448},{... | collective-permute-start | bytes 1769480 | tf_op jit(solution)/shard_map/ppermute | solution.py:210
  8.9 86.9 %all-to-all-start = ((bf16[64,3,8,1024]{3,2,1,0:T(8,128)(2,1)}), bf16[64,3,8,1024]{3,2,1,0:T(8,128)(2,1)S(1)}, u32[]{:S(2)}, u32[]{:S(2)}) async-start(bf16[64,3,8,1024]{3,2,1,0:T(8,128)(2,1)} %pack.1), calls=%async_computation | async-start | bytes 6291456 | tf_op jit(solution)/shard_map/all_to_all | solution.py:220
  23.3 1.1 copy-start.5
  24.3 18.2 %copy-start.2 = (s32[3,32,8]{1,2,0:T(8,128)S(1)}, s32[3,32,8]{1,2,0:T(8,128)}, u32[]{:S(2)}) copy-start(s32[3,32,8]{1,2,0:T(8,128)} %param.9) | copy-start | bytes 9220
  24.3 18.2 %copy-start.3 = (f32[3,32,8]{1,2,0:T(8,128)S(1)}, f32[3,32,8]{1,2,0:T(8,128)}, u32[]{:S(2)}) copy-start(f32[3,32,8]{1,2,0:T(8,128)} %param.10) | copy-start | bytes 9220
  25.5 3.9 %collective-permute-start.1 = (bf16[2,3,48,1024]{3,2,1,0:T(8,128)(2,1)S(1)}, bf16[2,3,48,1024]{3,2,1,0:T(8,128)(2,1)S(1)}, u32[]{:S(2)}, u32[]{:S(2)}) collective-permute-start(bf16[2,3,48,1024]{3,2,1,0:T(8,128)(2,1)S(1)} %get-tuple-element.20), channel_id=1, source_target_pairs={{0,32},{32,0},{64,96},{96,64},{128,160},{160,128},{192,224},{224,1... | collective-permute-start | bytes 1769480 | tf_op jit(solution)/shard_map/ppermute | solution.py:210
  30.5 32.6 %collective-permute-start.2 = (bf16[2,3,96,1024]{3,2,1,0:T(8,128)(2,1)}, bf16[2,3,96,1024]{3,2,1,0:T(8,128)(2,1)}, u32[]{:S(2)}, u32[]{:S(2)}) collective-permute-start(bf16[2,3,96,1024]{3,2,1,0:T(8,128)(2,1)} %join.1.refs_0_), channel_id=1, source_target_pairs={{0,128},{32,160},{64,192},{96,224},{128,0},{160,32},{192,64},{224,... | collective-permute-start | bytes 3538952 | tf_op jit(solution)/shard_map/ppermute | solution.py:210
  35.4 52.1 %collective-permute-start.3 = (bf16[2,3,96,1024]{3,2,1,0:T(8,128)(2,1)}, bf16[2,3,96,1024]{3,2,1,0:T(8,128)(2,1)}, u32[]{:S(2)}, u32[]{:S(2)}) collective-permute-start(bf16[2,3,96,1024]{3,2,1,0:T(8,128)(2,1)} %join.1.refs_0_), channel_id=1, source_target_pairs={{0,64},{32,96},{64,128},{96,160},{128,192},{160,224},{192,0},{224,... | collective-permute-start | bytes 3538952 | tf_op jit(solution)/shard_map/ppermute | solution.py:210
  38.0 49.7 %collective-permute-start.4 = (bf16[2,3,96,1024]{3,2,1,0:T(8,128)(2,1)}, bf16[2,3,96,1024]{3,2,1,0:T(8,128)(2,1)}, u32[]{:S(2)}, u32[]{:S(2)}) collective-permute-start(bf16[2,3,96,1024]{3,2,1,0:T(8,128)(2,1)} %join.1.refs_0_), channel_id=1, source_target_pairs={{0,192},{32,224},{64,0},{96,32},{128,64},{160,96},{192,128},{224,1... | collective-permute-start | bytes 3538952 | tf_op jit(solution)/shard_map/ppermute | solution.py:210
  43.1 52.6 %copy-start.4 = (s32[64]{0:T(128)S(1)}, s32[64]{0:T(128)}, u32[]{:S(2)}) copy-start(s32[64]{0:T(128)} %switch_ref.1) | copy-start | bytes 772
  90.0 2.1 %copy-start = (bf16[2,3,384,1024]{3,2,1,0:T(8,128)(2,1)}, bf16[2,3,384,1024]{3,2,1,0:T(8,128)(2,1)S(1)}, u32[]{:S(2)}) copy-start(bf16[2,3,384,1024]{3,2,1,0:T(8,128)(2,1)S(1)} %stage.1.weights_hbm) | copy-start | bytes 14155780
  103.0 84.3 %copy-start.1 = (bf16[3,32,1024]{2,1,0:T(8,128)(2,1)S(1)}, bf16[3,32,1024]{2,1,0:T(8,128)(2,1)}, u32[]{:S(2)}) copy-start(bf16[3,32,1024]{2,1,0:T(8,128)(2,1)} %hidden_ref.1) | copy-start | bytes 589828
